TPU v7x, 128 devices: a whole 4x4x4 slice. The times are simulated.
128 devices in a mesh: fsdp: 4 (over y_lo, core), context: 8 (over x, y_hi), tensor: 4 (over z).
Axes of the slice: x: 4, y: 4 (y_hi: 2, y_lo: 2; y = y_hi * 2 + y_lo), z: 4, core: 2. Of those that a mesh axis runs over, the one named last changes fastest.
Arguments:
- tokens: bfloat16 [4, 2048, 1152], P('fsdp', 'context'), may hold values from -6 to 6
- block_order: int32 [4, 16], P('fsdp'), may hold values from 0 to 15, each once within a row
- cotangent: bfloat16 [4, 2048, 1152], P('fsdp', 'context'), may hold values from -6 to 6
- w_query: bfloat16 [1152, 1024], P('fsdp', 'tensor'), may hold values from -0.1875 to 0.1875
- w_key: bfloat16 [1152, 256], P('fsdp'), may hold values from -0.1875 to 0.1875
- w_value: bfloat16 [1152, 256], P('fsdp'), may hold values from -0.1875 to 0.1875
- w_out: bfloat16 [1024, 1152], P('tensor', 'fsdp'), may hold values from -0.1875 to 0.1875
- w_gate: bfloat16 [1152, 6912], P('fsdp', 'tensor'), may hold values from -0.1875 to 0.1875
- w_up: bfloat16 [1152, 6912], P('fsdp', 'tensor'), may hold values from -0.1875 to 0.1875
- w_down: bfloat16 [6912, 1152], P('tensor', 'fsdp'), may hold values from -0.078125 to 0.078125
- gains: bfloat16 [4, 1152], P(None, 'fsdp'), may hold values from 0.5 to 1.5
- head_gains: bfloat16 [2, 256], P(None, 'fsdp'), may hold values from 0.5 to 1.5
Outputs:
- out: bfloat16 [4, 2048, 1152], P('fsdp', 'context')
- grad_tokens: float32 [4, 2048, 1152], P('fsdp', 'context')
- grad_w_query: float32 [1152, 1024], P('fsdp', 'tensor')
- grad_w_key: float32 [1152, 256], P('fsdp')
- grad_w_value: float32 [1152, 256], P('fsdp')
- grad_w_out: float32 [1024, 1152], P('tensor', 'fsdp')
- grad_w_gate: float32 [1152, 6912], P('fsdp', 'tensor')
- grad_w_up: float32 [1152, 6912], P('fsdp', 'tensor')
- grad_w_down: float32 [6912, 1152], P('tensor', 'fsdp')
- grad_gains: float32 [4, 1152], P(None, 'fsdp')
- grad_head_gains: float32 [2, 256], P(None, 'fsdp')
Inputs may be any that keep to these rules, and one draw needn't show every extreme that they name: `block_order`: each row lists every block number of its sequence once, in a seeded order.
All inputs are finite; a program needn't handle non-finite values.
Results may differ from a plain program's by a relative error of at most 0.03.
Values may be sent and summed in bfloat16 or wider, within the bound.
A program may use at most 128 MiB of HBM per device.

v0:
```python
import math

import jax
import jax.numpy as jnp
from jax import lax
from jax.sharding import PartitionSpec as P

HD = 256


ROPE_BASE = 1000000.0
EPS = 1e-06


def normalize(values, gain):
    return values * lax.rsqrt(jnp.mean(values * values, axis=-1, keepdims=True) + EPS) * gain


def rotate(values, cosine, sine):
    middle = values.shape[-1] // 2
    first = values[..., :middle]
    second = values[..., middle:]
    return jnp.concatenate(
        [first * cosine - second * sine, second * cosine + first * sine], axis=-1
    )


def tables(positions):
    steps = jnp.arange(HD // 2, dtype=jnp.float32) * (2.0 / HD)
    inverse = jnp.exp(-math.log(ROPE_BASE) * steps)
    angle = positions.astype(jnp.float32)[:, None] * inverse[None, :]
    return (jnp.cos(angle), jnp.sin(angle))


def plain(left, right):
    return jnp.dot(left, right, preferred_element_type=jnp.float32)


def inner(left, right):
    return lax.dot_general(
        left, right, (((0,), (0,)), ((), ())), preferred_element_type=jnp.float32
    )


def against(left, right):
    return lax.dot_general(
        left, right, (((1,), (1,)), ((), ())), preferred_element_type=jnp.float32
    )


def per_device(
    tokens,
    block_order,
    cotangent,
    w_query,
    w_key,
    w_value,
    w_out,
    w_gate,
    w_up,
    w_down,
    gains,
    head_gains,
):
    seq_dev, block_len, width = tokens.shape
    tok_rows = seq_dev * block_len
    cycle_size = lax.axis_size("context")
    cycle_index = lax.axis_index("context")
    share = tok_rows // lax.axis_size("tensor")
    share_start = lax.axis_index("tensor") * share
    span = block_len // 2
    seq_len = block_len * cycle_size
    scale = HD ** (-0.5)
    offsets = jnp.arange(seq_len, dtype=jnp.int32)
    pos_table = jnp.repeat(block_order, span, axis=1) * span + (offsets % span)[None, :]
    query_pos = lax.dynamic_slice_in_dim(pos_table, cycle_index * block_len, block_len, 1).reshape(
        tok_rows
    )
    query_seq = jnp.repeat(jnp.arange(seq_dev, dtype=jnp.int32), block_len)
    key_pos = pos_table.reshape(seq_dev, cycle_size, block_len).transpose(1, 0, 2).reshape(-1)
    key_seq = jnp.broadcast_to(
        jnp.arange(seq_dev, dtype=jnp.int32)[None, :, None], (cycle_size, seq_dev, block_len)
    ).reshape(-1)
    visible = ((key_seq[None, :] == query_seq[:, None]) & (key_pos[None, :] <= query_pos[:, None]))[
        :, None, :
    ]
    cosine, sine = tables(query_pos)
    gathered = (
        lax.all_gather(w_query, "fsdp", axis=0, tiled=True),
        lax.all_gather(w_key, "fsdp", axis=0, tiled=True),
        lax.all_gather(w_value, "fsdp", axis=0, tiled=True),
        lax.all_gather(w_out, "fsdp", axis=1, tiled=True),
        lax.all_gather(w_gate, "fsdp", axis=0, tiled=True),
        lax.all_gather(w_up, "fsdp", axis=0, tiled=True),
        lax.all_gather(w_down, "fsdp", axis=1, tiled=True),
        lax.all_gather(gains, "fsdp", axis=1, tiled=True),
        lax.all_gather(head_gains, "fsdp", axis=1, tiled=True),
    )
    full_q, full_k, full_v, full_o, full_gate, full_up, full_down, full_gains, full_heads = gathered
    gain_rows = full_gains.astype(jnp.float32)
    head_rows = full_heads.astype(jnp.float32)
    num_heads = full_q.shape[1] // HD
    stream = tokens.reshape(tok_rows, width).astype(jnp.float32)
    upstream = cotangent.reshape(tok_rows, width).astype(jnp.float32)
    normed_f, pre_back = jax.vjp(normalize, stream, gain_rows[0])
    normed = normed_f.astype(jnp.bfloat16)
    q_proj = plain(normed, full_q)
    k_proj = plain(normed, full_k)
    values = plain(normed, full_v).astype(jnp.bfloat16)

    def query_prep(q_flat, q_gain):
        return rotate(
            normalize(q_flat.reshape(tok_rows, num_heads, HD), q_gain),
            cosine[:, None, :],
            sine[:, None, :],
        )

    q_float, query_back = jax.vjp(query_prep, q_proj, head_rows[0])
    queries = q_float.astype(jnp.bfloat16)
    keys = rotate(normalize(k_proj, head_rows[1]), cosine, sine).astype(jnp.bfloat16)
    keys_all, values_all = (
        lax.all_gather(keys, "context", axis=0, tiled=True),
        lax.all_gather(values, "context", axis=0, tiled=True),
    )
    scores = (
        jnp.einsum("qhd,kd->qhk", queries, keys_all, preferred_element_type=jnp.float32) * scale
    )
    top = jnp.max(jnp.where(visible, scores, -1e30), axis=-1, keepdims=True)
    total = jnp.sum(jnp.where(visible, jnp.exp(scores - top), 0.0), axis=-1, keepdims=True)
    lse = top + jnp.log(total)
    probs = jnp.where(visible, jnp.exp(scores - lse), 0.0)
    probs_low = probs.astype(jnp.bfloat16)
    attn = jnp.einsum(
        "qhk,kd->qhd", probs_low, values_all, preferred_element_type=jnp.float32
    ).astype(jnp.bfloat16)
    attn_flat = attn.reshape(tok_rows, num_heads * HD)
    branch = lax.psum(plain(attn_flat, full_o), "tensor")
    branch_norm, post_back = jax.vjp(normalize, branch, gain_rows[1])
    middle = stream + branch_norm
    normed_two_f, pre_two_back = jax.vjp(normalize, middle, gain_rows[2])
    normed_two = normed_two_f.astype(jnp.bfloat16)
    gate = plain(normed_two, full_gate)
    up_part = plain(normed_two, full_up)

    def geglu(gate_in, up_in):
        return jax.nn.gelu(gate_in, approximate=True) * up_in

    hidden_f, geglu_back = jax.vjp(geglu, gate, up_part)
    hidden = hidden_f.astype(jnp.bfloat16)
    ffn = lax.psum(plain(hidden, full_down).astype(jnp.bfloat16), "tensor").astype(jnp.float32)
    ffn_norm, post_two_back = jax.vjp(normalize, ffn, gain_rows[3])
    result_rows = (middle + ffn_norm).astype(jnp.bfloat16)
    d_ffn, d_gain_three = post_two_back(upstream)
    d_ffn_low = d_ffn.astype(jnp.bfloat16)
    gain_three_part = jnp.zeros((width,), jnp.float32)
    result = result_rows.reshape(seq_dev, block_len, width)
    grad_down = inner(hidden, d_ffn_low)
    d_hidden = against(d_ffn_low, full_down)
    d_gate, d_up = geglu_back(d_hidden)
    d_gate_low = d_gate.astype(jnp.bfloat16)
    d_up_low = d_up.astype(jnp.bfloat16)
    grad_gate = inner(normed_two, d_gate_low)
    grad_up = inner(normed_two, d_up_low)
    d_normed_two = lax.psum(
        (against(d_gate_low, full_gate) + against(d_up_low, full_up)).astype(jnp.bfloat16), "tensor"
    ).astype(jnp.float32)
    d_middle_norm, d_gain_two = pre_two_back(d_normed_two)
    d_middle = upstream + d_middle_norm
    d_branch, d_gain_one = post_back(d_middle)
    d_branch_low = d_branch.astype(jnp.bfloat16)
    grad_out = inner(attn_flat, d_branch_low)
    d_attn = against(d_branch_low, full_o).astype(jnp.bfloat16).reshape(tok_rows, num_heads, HD)
    d_probs = jnp.einsum("qhd,kd->qhk", d_attn, values_all, preferred_element_type=jnp.float32)
    delta = jnp.sum(probs * d_probs, axis=-1, keepdims=True)
    d_scores = (probs * (d_probs - delta)).astype(jnp.bfloat16)
    d_queries = (
        jnp.einsum("qhk,kd->qhd", d_scores, keys_all, preferred_element_type=jnp.float32) * scale
    )
    d_key_part = (
        jnp.einsum("qhk,qhd->kd", d_scores, queries, preferred_element_type=jnp.float32) * scale
    )
    d_value_part = jnp.einsum("qhk,qhd->kd", probs_low, d_attn, preferred_element_type=jnp.float32)
    kv_grads = lax.psum_scatter(
        jnp.concatenate([d_key_part, d_value_part], axis=1).astype(jnp.bfloat16),
        ("context", "tensor"),
        scatter_dimension=0,
        tiled=True,
    ).astype(jnp.float32)
    d_keys = kv_grads[:, :HD]
    d_values_low = kv_grads[:, HD:].astype(jnp.bfloat16)
    k_slice = lax.dynamic_slice_in_dim(k_proj, share_start, share, 0)
    cos_slice = lax.dynamic_slice_in_dim(cosine, share_start, share, 0)
    sin_slice = lax.dynamic_slice_in_dim(sine, share_start, share, 0)
    normed_slice = lax.dynamic_slice_in_dim(normed, share_start, share, 0)

    def key_prep(k_in, k_gain):
        return rotate(normalize(k_in, k_gain), cos_slice, sin_slice)

    key_unused, key_back = jax.vjp(key_prep, k_slice, head_rows[1])
    d_k_proj, d_key_gain = key_back(d_keys)
    d_k_low = d_k_proj.astype(jnp.bfloat16)
    grad_key = inner(normed_slice, d_k_low)
    grad_value = inner(normed_slice, d_values_low)
    d_normed_kv = against(d_k_low, full_k) + against(d_values_low, full_v)
    placed = lax.dynamic_update_slice_in_dim(
        jnp.zeros((tok_rows, width), jnp.float32), d_normed_kv, share_start, 0
    )
    d_q_proj, d_query_gain = query_back(d_queries)
    d_q_low = d_q_proj.astype(jnp.bfloat16)
    grad_query = inner(normed, d_q_low)
    d_normed = lax.psum((against(d_q_low, full_q) + placed).astype(jnp.bfloat16), "tensor").astype(
        jnp.float32
    )
    d_stream_norm, d_gain_zero = pre_back(d_normed)
    grad_stream = (d_middle + d_stream_norm).reshape(seq_dev, block_len, width)
    head_grad = jnp.stack([d_query_gain, d_key_gain])
    key_sum, value_sum, head_sum, three_sum = (
        lax.psum(grad_key.astype(jnp.bfloat16), "tensor").astype(jnp.float32),
        lax.psum(grad_value.astype(jnp.bfloat16), "tensor").astype(jnp.float32),
        lax.psum(head_grad.astype(jnp.bfloat16), "tensor").astype(jnp.float32),
        lax.psum(gain_three_part.astype(jnp.bfloat16), "tensor").astype(jnp.float32),
    )
    gain_grad = jnp.stack([d_gain_zero, d_gain_one, d_gain_two, d_gain_three + three_sum])
    owned = (
        lax.psum_scatter(
            grad_query.astype(jnp.bfloat16), "fsdp", scatter_dimension=0, tiled=True
        ).astype(jnp.float32),
        lax.psum_scatter(
            key_sum.astype(jnp.bfloat16), "fsdp", scatter_dimension=0, tiled=True
        ).astype(jnp.float32),
        lax.psum_scatter(
            value_sum.astype(jnp.bfloat16), "fsdp", scatter_dimension=0, tiled=True
        ).astype(jnp.float32),
        lax.psum_scatter(
            grad_out.astype(jnp.bfloat16), "fsdp", scatter_dimension=1, tiled=True
        ).astype(jnp.float32),
        lax.psum_scatter(
            grad_gate.astype(jnp.bfloat16), "fsdp", scatter_dimension=0, tiled=True
        ).astype(jnp.float32),
        lax.psum_scatter(
            grad_up.astype(jnp.bfloat16), "fsdp", scatter_dimension=0, tiled=True
        ).astype(jnp.float32),
        lax.psum_scatter(
            grad_down.astype(jnp.bfloat16), "fsdp", scatter_dimension=1, tiled=True
        ).astype(jnp.float32),
        lax.psum_scatter(
            gain_grad.astype(jnp.bfloat16), "fsdp", scatter_dimension=1, tiled=True
        ).astype(jnp.float32),
        lax.psum_scatter(
            head_sum.astype(jnp.bfloat16), "fsdp", scatter_dimension=1, tiled=True
        ).astype(jnp.float32),
    )
    summed = (
        lax.psum(owned[0].astype(jnp.bfloat16), "context").astype(jnp.float32),
        lax.psum(owned[1].astype(jnp.bfloat16), "context").astype(jnp.float32),
        lax.psum(owned[2].astype(jnp.bfloat16), "context").astype(jnp.float32),
        lax.psum(owned[3].astype(jnp.bfloat16), "context").astype(jnp.float32),
        lax.psum(owned[4].astype(jnp.bfloat16), "context").astype(jnp.float32),
        lax.psum(owned[5].astype(jnp.bfloat16), "context").astype(jnp.float32),
        lax.psum(owned[6].astype(jnp.bfloat16), "context").astype(jnp.float32),
        lax.psum(owned[7].astype(jnp.bfloat16), "context").astype(jnp.float32),
        lax.psum(owned[8].astype(jnp.bfloat16), "context").astype(jnp.float32),
    )
    sum_q, sum_k, sum_v, sum_o, sum_gate, sum_up, sum_down, sum_gains, sum_heads = summed
    return (
        result,
        grad_stream,
        sum_q,
        sum_k,
        sum_v,
        sum_o,
        sum_gate,
        sum_up,
        sum_down,
        sum_gains,
        sum_heads,
    )


def solution(mesh):
    in_specs = (
        P("fsdp", "context", None),
        P("fsdp", None),
        P("fsdp", "context", None),
        P("fsdp", "tensor"),
        P("fsdp", None),
        P("fsdp", None),
        P("tensor", "fsdp"),
        P("fsdp", "tensor"),
        P("fsdp", "tensor"),
        P("tensor", "fsdp"),
        P(None, "fsdp"),
        P(None, "fsdp"),
    )
    out_specs = (
        P("fsdp", "context", None),
        P("fsdp", "context", None),
        P("fsdp", "tensor"),
        P("fsdp", None),
        P("fsdp", None),
        P("tensor", "fsdp"),
        P("fsdp", "tensor"),
        P("fsdp", "tensor"),
        P("tensor", "fsdp"),
        P(None, "fsdp"),
        P(None, "fsdp"),
    )
    return jax.shard_map(
        per_device, mesh=mesh, in_specs=in_specs, out_specs=out_specs, check_vma=False
    )
```

profile of v0, /device:TPU:0, one launch (start us, length us, event | category | flops | bytes accessed | tf_op | source)
XLA Modules:
  0.0 1008.6 jit_solution(14156548701741168550)
XLA Ops:
  15.6 7.9 all_gather.36
  32.2 7.6 all_gather.38
  41.8 9.0 all_gather.34
  51.7 8.1 all_gather.40
  60.5 22.4 %all-gather.8.cloned.1.call-done = bf16[2048,256]{1,0:T(8,128)(2,1)} async-done(((bf16[256,256]{1,0:T(8,128)(2,1)}), bf16[2048,256]{1,0:T(8,128)(2,1)}) %all-gather.8.cloned.1.call-update) | async-done | bytes 1048592 | tf_op jit(solution)/shard_map/all_gather | solution.py:122
  85.9 46.0 %all-gather.10.cloned.1.call-done = bf16[2048,256]{1,0:T(8,128)(2,1)} async-done(((bf16[256,256]{1,0:T(8,128)(2,1)}), bf16[2048,256]{1,0:T(8,128)(2,1)}) %all-gather.10.cloned.1.call-update) | async-done | bytes 1048592 | tf_op jit(solution)/shard_map/all_gather | solution.py:123
  137.1 43.9 %all-reduce.13.cloned.1.call-done = f32[256,1152]{1,0:T(8,128)} async-done(((f32[256,1152]{1,0:T(8,128)}), f32[256,1152]{1,0:T(8,128)}) %all-reduce.13.cloned.1.call-update) | async-done | bytes 1179664 | tf_op jit(solution)/shard_map/psum | solution.py:137
  192.6 37.0 %all-gather.14.cloned.1.call-done = bf16[1152,1728]{1,0:T(8,128)(2,1)} async-done(((bf16[288,1728]{1,0:T(8,128)(2,1)}), bf16[1152,1728]{1,0:T(8,128)(2,1)}) %all-gather.14.cloned.1.call-update) | async-done | bytes 3981328 | tf_op jit(solution)/shard_map/all_gather | solution.py:94
  229.6 6.4 multiply_convert_fusion.2
  236.0 41.9 %all-gather.16.cloned.1.call-done = bf16[1728,1152]{0,1:T(8,128)(2,1)} async-done(((bf16[1728,288]{0,1:T(8,128)(2,1)}), bf16[1728,1152]{0,1:T(8,128)(2,1)}) %all-gather.16.cloned.1.call-update) | async-done | bytes 3981328 | tf_op jit(solution)/shard_map/all_gather | solution.py:95
  282.6 45.2 %all-reduce.15.cloned.1.call-done = bf16[256,1152]{1,0:T(8,128)(2,1)} async-done(((bf16[256,1152]{1,0:T(8,128)(2,1)}), bf16[256,1152]{1,0:T(8,128)(2,1)}) %all-reduce.15.cloned.1.call-update) | async-done | bytes 589840 | tf_op jit(solution)/shard_map/psum | solution.py:150
  331.6 7.2 multiply_convert_fusion.1
  344.2 43.9 %all-reduce.17.cloned.1.call-done = bf16[256,1152]{1,0:T(8,128)(2,1)} async-done(((bf16[256,1152]{1,0:T(8,128)(2,1)}), bf16[256,1152]{1,0:T(8,128)(2,1)}) %all-reduce.17.cloned.1.call-update) | async-done | bytes 589840 | tf_op jit(solution)/shard_map/psum | solution.py:164
  402.7 187.2 %reduce-scatter.15.cloned.1.call-done = bf16[64,512]{1,0:T(8,128)(2,1)} async-done(((bf16[2048,512]{1,0:T(8,128)(2,1)}), bf16[64,512]{1,0:T(8,128)(2,1)}) %reduce-scatter.15.cloned.1.call-update) | async-done | bytes 65552 | tf_op jit(solution)/shard_map/reduce_scatter | solution.py:183
  606.5 21.7 %reduce-scatter.29.cloned.1.call-done = bf16[288,256]{1,0:T(8,128)(2,1)} async-done(((bf16[1152,256]{1,0:T(8,128)(2,1)}), bf16[288,256]{1,0:T(8,128)(2,1)}) %reduce-scatter.29.cloned.1.call-update) | async-done | bytes 147472 | tf_op jit(solution)/shard_map/reduce_scatter | solution.py:231
  645.3 29.5 %all-reduce.21.cloned.1.call-done = (bf16[256,1152]{1,0:T(8,128)(2,1)}, bf16[288,256]{1,0:T(8,128)(2,1)}, bf16[288,256]{1,0:T(8,128)(2,1)}) async-done(((bf16[256,1152]{1,0:T(8,128)(2,1)}, bf16[288,256]{1,0:T(8,128)(2,1)}, bf16[288,256]{1,0:T(8,128)(2,1)}), (bf16[256,1152]{1,0:T(8,128)(2,1)}, bf16[288,256]{1,0:T(8,128)(2,1)}, bf16[288,256]{1,0:T(8,128)(2,1)})) %all-reduce.21.cloned.1.call-update) | async-done | bytes 884752 | tf_op jit(solution)/shard_map/psum | solution.py:211
  677.5 43.3 %reduce-scatter.25.cloned.1.call-done = bf16[1728,288]{0,1:T(8,128)(2,1)} async-done(((bf16[1728,1152]{0,1:T(8,128)(2,1)}), bf16[1728,288]{0,1:T(8,128)(2,1)}) %reduce-scatter.25.cloned.1.call-update) | async-done | bytes 995344 | tf_op jit(solution)/shard_map/reduce_scatter | solution.py:243
  720.8 47.9 %reduce-scatter.21.cloned.1.call-done = bf16[288,1728]{1,0:T(8,128)(2,1)} async-done(((bf16[1152,1728]{1,0:T(8,128)(2,1)}), bf16[288,1728]{1,0:T(8,128)(2,1)}) %reduce-scatter.21.cloned.1.call-update) | async-done | bytes 995344 | tf_op jit(solution)/shard_map/reduce_scatter | solution.py:237
  768.7 48.2 %reduce-scatter.23.cloned.1.call-done = bf16[288,1728]{1,0:T(8,128)(2,1)} async-done(((bf16[1152,1728]{1,0:T(8,128)(2,1)}), bf16[288,1728]{1,0:T(8,128)(2,1)}) %reduce-scatter.23.cloned.1.call-update) | async-done | bytes 995344 | tf_op jit(solution)/shard_map/reduce_scatter | solution.py:240
  816.9 34.6 %reduce-scatter.33.cloned.1.call-done = bf16[64,2]{1,0:T(8,128)(2,1)} async-done(((bf16[256,2]{1,0:T(8,128)(2,1)}), bf16[64,2]{1,0:T(8,128)(2,1)}) %reduce-scatter.33.cloned.1.call-update) | async-done | bytes 272
  852.3 10.7 %psum.133 = bf16[2,64]{1,0:T(2,128)(2,1)S(1)} all-reduce(bf16[2,64]{1,0:T(2,128)(2,1)S(1)} %copy.47), channel_id=1, replica_groups=mesh['fsdp'=4,'context'=8,'tensor'=4] {'tensor'}, use_global_device_ids=true, to_apply=%region_45.46 | all-reduce | flops 128 | bytes 512 | tf_op jit(solution)/shard_map/psum | solution.py:220
  864.4 38.0 %reduce-scatter.31.cloned.1.call-done = bf16[288,4]{1,0:T(8,128)(2,1)} async-done(((bf16[1152,4]{1,0:T(8,128)(2,1)}), bf16[288,4]{1,0:T(8,128)(2,1)}) %reduce-scatter.31.cloned.1.call-update) | async-done | bytes 2320
  903.4 25.3 %all-reduce.4 = (bf16[4,288]{1,0:T(4,128)(2,1)S(1)}, bf16[2,64]{1,0:T(2,128)(2,1)S(1)}) all-reduce(bf16[4,288]{1,0:T(4,128)(2,1)S(1)} %copy.45, bf16[2,64]{1,0:T(2,128)(2,1)S(1)} %psum.133), channel_id=1, replica_groups=mesh['fsdp'=4,'context'=8,'tensor'=4] {'context'}, use_global_device_ids=true, to_apply=%region_42.43 | all-reduce | flops 1280 | bytes 5120 | tf_op jit(solution)/shard_map/psum | solution.py:261
  929.9 62.5 %all-reduce.19.cloned.1.call-done = (bf16[288,256]{1,0:T(8,128)(2,1)}, bf16[288,256]{1,0:T(8,128)(2,1)}, bf16[288,256]{1,0:T(8,128)(2,1)}, bf16[256,288]{0,1:T(8...) async-done(((bf16[288,256]{1,0:T(8,128)(2,1)}, bf16[288,256]{1,0:T(8,128)(2,1)}, bf16[288,256]{1,0:T(8,128)(2,1)}, ...) | async-done | bytes 3575824 | tf_op jit(solution)/shard_map/psum | solution.py:254
  (359 shorter events, 116.2 us)
Async XLA Ops:
  8.0 74.8 %all-gather.8.cloned.1.call-start = ((), (), s32[]{:S(2)}) async-start(), calls=%async_computation.10 | async-start | bytes 1179648 | tf_op jit(solution)/shard_map/all_gather | solution.py:122
  30.0 55.3 %copy-start.60 = (s32[1,256]{1,0:T(1,128)}, s32[1,256]{1,0:T(1,128)S(1)}, u32[]{:S(2)}) copy-start(s32[1,256]{1,0:T(1,128)S(1)} %fusion.79) | copy-start | bytes 3076
  32.1 99.8 %all-gather.10.cloned.1.call-start = ((), (), s32[]{:S(2)}) async-start(), calls=%async_computation.11 | async-start | bytes 1179648 | tf_op jit(solution)/shard_map/all_gather | solution.py:123
  41.7 139.3 %all-reduce.13.cloned.1.call-start = ((), (), s32[]{:S(2)}) async-start(), calls=%async_computation.12 | async-start | bytes 2359296 | tf_op jit(solution)/shard_map/psum | solution.py:137
  135.1 52.2 %all-gather.12.cloned.1.call-start = ((), (), s32[]{:S(2)}) async-start(), calls=%async_computation.13 | async-start | bytes 5160960 | tf_op jit(solution)/shard_map/all_gather | solution.py:93
  135.7 93.9 %all-gather.14.cloned.1.call-start = ((), (), s32[]{:S(2)}) async-start(), calls=%async_computation.14 | async-start | bytes 5160960 | tf_op jit(solution)/shard_map/all_gather | solution.py:94
  136.3 141.6 %all-gather.16.cloned.1.call-start = ((), (), s32[]{:S(2)}) async-start(), calls=%async_computation.15 | async-start | bytes 5160960 | tf_op jit(solution)/shard_map/all_gather | solution.py:95
  136.9 190.9 %all-reduce.15.cloned.1.call-start = ((), (), s32[]{:S(2)}) async-start(), calls=%async_computation.16 | async-start | bytes 1179648 | tf_op jit(solution)/shard_map/psum | solution.py:150
  282.6 105.5 %all-reduce.17.cloned.1.call-start = ((), (), s32[]{:S(2)}) async-start(), calls=%async_computation.17 | async-start | bytes 1179648 | tf_op jit(solution)/shard_map/psum | solution.py:164
  343.9 246.1 %reduce-scatter.15.cloned.1.call-start = ((), (), s32[]{:S(2)}) async-start(), calls=%async_computation.18 | async-start | bytes 2162688 | tf_op jit(solution)/shard_map/reduce_scatter | solution.py:183
  401.7 189.9 %copy-start.63 = (f32[1,256]{1,0:T(1,128)S(1)}, f32[1,256]{1,0:T(1,128)}, u32[]{:S(2)}) copy-start(f32[1,256]{1,0:T(1,128)} %copy-done.62) | copy-start | bytes 3076
  401.7 190.6 %copy-start.6 = (bf16[256,1152]{1,0:T(8,128)(2,1)S(1)}, bf16[256,1152]{1,0:T(8,128)(2,1)}, u32[]{:S(2)}) copy-start(bf16[256,1152]{1,0:T(8,128)(2,1)} %copy-done.5) | copy-start | bytes 1769476
  401.7 204.8 %reduce-scatter.27.cloned.1.call-start = ((), (), s32[]{:S(2)}) async-start(), calls=%async_computation.24 | async-start | bytes 737280 | tf_op jit(solution)/shard_map/reduce_scatter | solution.py:228
  402.7 190.8 %copy-start.92 = (f32[64]{0:T(128)}, f32[64]{0:T(128)S(1)}, u32[]{:S(2)}) copy-start(f32[64]{0:T(128)S(1)} %fusion.85) | copy-start | bytes 772
  593.5 34.7 %reduce-scatter.29.cloned.1.call-start = ((), (), s32[]{:S(2)}) async-start(), calls=%async_computation.25 | async-start | bytes 737280 | tf_op jit(solution)/shard_map/reduce_scatter | solution.py:231
  597.9 76.9 %all-reduce.21.cloned.1.call-start = ((), (), s32[]{:S(2)}) async-start(), calls=%async_computation.29 | async-start | bytes 1769472 | tf_op jit(solution)/shard_map/psum | solution.py:211
  628.3 49.2 %reduce-scatter.19.cloned.1.call-start = ((), (), s32[]{:S(2)}) async-start(), calls=%async_computation.20 | async-start | bytes 737280 | tf_op jit(solution)/shard_map/reduce_scatter | solution.py:234
  629.6 47.9 %reduce-scatter.17.cloned.1.call-start = ((), (), s32[]{:S(2)}) async-start(), calls=%async_computation.19 | async-start | bytes 737280 | tf_op jit(solution)/shard_map/reduce_scatter | solution.py:225
  630.9 89.8 %reduce-scatter.25.cloned.1.call-start = ((), (), s32[]{:S(2)}) async-start(), calls=%async_computation.23 | async-start | bytes 5160960 | tf_op jit(solution)/shard_map/reduce_scatter | solution.py:243
  634.5 134.1 %reduce-scatter.21.cloned.1.call-start = ((), (), s32[]{:S(2)}) async-start(), calls=%async_computation.21 | async-start | bytes 5160960 | tf_op jit(solution)/shard_map/reduce_scatter | solution.py:237
  639.2 177.7 %reduce-scatter.23.cloned.1.call-start = ((), (), s32[]{:S(2)}) async-start(), calls=%async_computation.22 | async-start | bytes 5160960 | tf_op jit(solution)/shard_map/reduce_scatter | solution.py:240
  643.7 207.9 %reduce-scatter.33.cloned.1.call-start = ((), (), s32[]{:S(2)}) async-start(), calls=%async_computation.27 | async-start | bytes 81920
  645.2 257.2 %reduce-scatter.31.cloned.1.call-start = ((), (), s32[]{:S(2)}) async-start(), calls=%async_computation.26 | async-start | bytes 368640
  677.4 315.0 %all-reduce.19.cloned.1.call-start = ((), (), s32[]{:S(2)}) async-start(), calls=%async_computation.28 | async-start | bytes 7372800 | tf_op jit(solution)/shard_map/psum | solution.py:254
  (102 other events, 878.9 us)
Sparse Core Ops, SparseCore 0:
  32.3 50.5 all-gather.7
  85.7 46.1 all-gather.9
  135.2 45.6 all-reduce.12
  282.7 45.0 all-reduce.14
  344.0 44.0 all-reduce.16
  401.8 188.0 reduce-scatter.14
  628.3 46.4 all-reduce.20
  817.0 175.2 all-reduce.18
Sparse Core Ops, SparseCore 1:
  137.2 44.1 all-gather.11
  182.9 46.6 all-gather.13
  231.2 46.6 all-gather.15
  593.6 12.8 reduce-scatter.26
  609.0 19.1 reduce-scatter.28
  631.6 19.2 reduce-scatter.18
  653.2 19.4 reduce-scatter.16
  675.1 45.7 reduce-scatter.24
  723.1 45.5 reduce-scatter.20
  771.3 45.6 reduce-scatter.22
  819.7 31.8 reduce-scatter.32
  854.6 47.7 reduce-scatter.30
where the time goes:
time: 1010 us
  waiting for transfers between devices  801 us (79%)
  blocking collectives  79.1 us (8%)
  matrix products  53.7 us (5%)
  other arithmetic  39.7 us (4%)
  between operations  16.9 us (2%)
  local copies, waits for them, and re-layouts  16.4 us (2%)
    reduce_scatter x1, waiting for transfers between devices, per_device(): lax.psum_scatter(jnp.concatenate([d_key_part, d_value_part], axis=1).asty...  187 us
    unnamed x22, waiting for transfers between devices  74.5 us
    psum x1, waiting for transfers between devices, per_device(): lax.psum(owned[0].astype(jnp.bfloat16), 'context').astype(jnp.float32)  62.5 us
    reduce_scatter x1, waiting for transfers between devices, per_device(): lax.psum_scatter(grad_up.astype(jnp.bfloat16), 'fsdp', scatter_dimension=...  48.2 us
    reduce_scatter x1, waiting for transfers between devices, per_device(): lax.psum_scatter(grad_gate.astype(jnp.bfloat16), 'fsdp', scatter_dimensio...  47.9 us
    all_gather x1, waiting for transfers between devices, per_device(): lax.all_gather(values, 'context', axis=0, tiled=True)  46 us
    psum x1, waiting for transfers between devices, per_device(): lax.psum(plain(hidden, full_down).astype(jnp.bfloat16), 'tensor')  45.2 us
    psum x1, waiting for transfers between devices, per_device(): lax.psum((against(d_gate_low, full_gate) + against(d_up_low, full_up)).as...  43.9 us
  transfers between devices with their start and end apart: 20, of which 17 were waited for; matrix products, arithmetic and copies ran while one was open for 5% of the time, Pallas kernels for 0%

commit v1 on v0

v1 whole, which is shorter than its diff:
```python
import functools
import math

import jax
import jax.numpy as jnp
from jax import lax
from jax.experimental import pallas as pl
from jax.experimental.pallas import tpu as pltpu
from jax.sharding import PartitionSpec as P

HD = 256
ROPE_BASE = 1000000.0
EPS = 1e-06
MESH = pl.DeviceIdType.MESH
BF = jnp.bfloat16
F32 = jnp.float32


def normalize(values, gain):
    return values * lax.rsqrt(jnp.mean(values * values, axis=-1, keepdims=True) + EPS) * gain


def rotate(values, cosine, sine):
    middle = values.shape[-1] // 2
    first = values[..., :middle]
    second = values[..., middle:]
    return jnp.concatenate(
        [first * cosine - second * sine, second * cosine + first * sine], axis=-1
    )


def tables(positions):
    steps = jnp.arange(HD // 2, dtype=jnp.float32) * (2.0 / HD)
    inverse = jnp.exp(-math.log(ROPE_BASE) * steps)
    angle = positions.astype(jnp.float32)[:, None] * inverse[None, :]
    return (jnp.cos(angle), jnp.sin(angle))


def plain(left, right):
    return jnp.dot(left, right, preferred_element_type=jnp.float32)


def inner(left, right):
    return lax.dot_general(
        left, right, (((0,), (0,)), ((), ())), preferred_element_type=jnp.float32
    )


def against(left, right):
    return lax.dot_general(
        left, right, (((1,), (1,)), ((), ())), preferred_element_type=jnp.float32
    )


class Place:
    def __init__(self):
        f = lax.axis_index("fsdp")
        c = lax.axis_index("context")
        self.f, self.c, self.z = f, c, lax.axis_index("tensor")
        self.ylo, self.core = f // 2, f % 2
        self.x, self.yhi = c // 2, c % 2
        self.y = self.yhi * 2 + self.ylo

    def at(self, x=None, y=None, z=None, core=None):
        x = self.x if x is None else x
        y = self.y if y is None else y
        z = self.z if z is None else z
        core = self.core if core is None else core
        return ((y % 2) * 2 + core, x * 2 + y // 2, z)

    def sib(self):
        return self.at(core=1 - self.core)

    def dy(self, d):
        return self.at(y=(self.y + d) % 4)

    def dx(self, d):
        return self.at(x=(self.x + d) % 4)

    def dz(self, d):
        return self.at(z=(self.z + d) % 4)

    def dc(self, d):
        return (self.f, (self.c + d) % 8, self.z)

    def dcz(self, d):
        to = (self.c * 4 + self.z + d) % 32
        return (self.f, to // 4, to % 4)


def greet(devices):
    barrier = pltpu.get_barrier_semaphore()
    for device in devices:
        pl.semaphore_signal(barrier, inc=1, device_id=device, device_id_type=MESH)
    pl.semaphore_wait(barrier, len(devices))


def send(src, dst, ssem, rsem, device):
    copy = pltpu.make_async_remote_copy(
        src_ref=src, dst_ref=dst, send_sem=ssem, recv_sem=rsem, device_id=device, device_id_type=MESH
    )
    copy.start()
    return copy


def sems(n):
    return [pltpu.SemaphoreType.DMA((n,)), pltpu.SemaphoreType.DMA((n,))]


VM = pl.BlockSpec(memory_space=pltpu.VMEM)


def params(cid, limit=48):
    return pltpu.CompilerParams(
        collective_id=cid, has_side_effects=True, vmem_limit_bytes=limit * 2**20
    )


class Gather:
    def __init__(self, place, src, out, local, ssem, rsem, base):
        self.p, self.src, self.out = place, src, out
        self.local, self.ssem, self.rsem, self.base = local, ssem, rsem, base
        self.rows = src.shape[0]

    def start(self):
        p, rows, b = self.p, self.rows, self.base
        mine = pl.multiple_of(p.f * rows, rows)
        own = self.out.at[pl.ds(mine, rows)]
        s, r = self.ssem, self.rsem
        self.s = send(self.src, own, s.at[b + 2], r.at[b + 2], p.sib())
        self.l = pltpu.make_async_copy(self.src, own, self.local)
        self.l.start()

    def start_far(self):
        p, rows, half, b = self.p, self.rows, self.rows // 2, self.base
        first = self.out.at[pl.ds(pl.multiple_of(p.f * rows, half), half)]
        second = self.out.at[pl.ds(pl.multiple_of(p.f * rows + half, half), half)]
        s, r = self.ssem, self.rsem
        self.y = [
            send(self.src.at[pl.ds(0, half)], first, s.at[b], r.at[b], p.dy(1)),
            send(self.src.at[pl.ds(half, half)], second, s.at[b + 1], r.at[b + 1], p.dy(-1 + 4)),
        ]

    def forward(self):
        p, rows, b = self.p, self.rows, self.base
        for copy in self.y:
            copy.wait_recv()
        block = self.out.at[pl.ds(pl.multiple_of((2 * (1 - p.ylo) + p.core) * rows, rows), rows)]
        self.t = send(block, block, self.ssem.at[b + 3], self.rsem.at[b + 3], p.sib())

    def finish(self):
        self.l.wait()
        for copy in self.y:
            copy.wait_send()
        self.s.wait()
        self.t.wait()


class ZSum:
    def __init__(self, place, x, got, out, s1, r1, s2, r2):
        self.p, self.x, self.got, self.out = place, x, got, out
        self.s1, self.r1, self.s2, self.r2 = s1, r1, s2, r2

    def rows(self, block):
        return pl.ds(pl.multiple_of(block * 64, 64), 64)

    def start(self):
        p = self.p
        self.c1 = [
            send(
                self.x.at[self.rows((p.z + d) % 4)],
                self.got.at[d - 1],
                self.s1.at[d - 1],
                self.r1.at[d - 1],
                p.dz(d),
            )
            for d in (2, 1, 3)
        ]

    def middle(self):
        p = self.p
        for copy in self.c1:
            copy.wait_recv()
        own = self.rows(p.z)

        @pl.loop(0, 4)
        def _(i):
            at = pl.ds(pl.multiple_of(p.z * 64 + i * 16, 16), 16)
            to = pl.ds(pl.multiple_of(i * 16, 16), 16)
            total = self.x[at, :].astype(F32)
            for d in range(3):
                total = total + self.got[d, to, :].astype(F32)
            self.out[at, :] = total.astype(BF)

        self.c2 = [
            send(self.out.at[own], self.out.at[own], self.s2.at[d - 1], self.r2.at[d - 1], p.dz(d))
            for d in (2, 1, 3)
        ]

    def finish(self):
        for copy in self.c1:
            copy.wait_send()
        for copy in self.c2:
            copy.wait()


class Reduce:
    def __init__(self, place, out, bufs, cut, src=None, left=None, right=None):
        self.p, self.src, self.left, self.right = place, src, left, right
        self.out, self.cut = out, cut
        if src is None:
            self.sent, bufs = bufs[0], bufs[1:]
        self.r1, self.r2, self.q, self.r3, self.r4, self.r5, self.s, self.r = bufs
        self.n = out.shape[1]
        self.ns = 0

    def go(self, src, dst, device):
        i = self.ns
        self.ns += 1
        return send(src, dst, self.s.at[i], self.r.at[i], device)

    def rows(self, block):
        return pl.ds(pl.multiple_of(block * 288, 16), 288)

    def product(self, block, c0, c1):
        return plain(self.left[self.rows(block), :], self.right[:, c0:c1])

    def tiles(self):
        return [(c0, min(c0 + 256, self.n)) for c0 in range(0, self.n, 256)]

    def one(self):
        p = self.p
        if self.src is None:

            @pl.loop(0, 2)
            def _(j):
                for c0, c1 in self.tiles():
                    self.sent[j, :, c0:c1] = self.product(2 * j + 1 - p.core, c0, c1).astype(BF)

            blocks = [self.sent.at[j] for j in (0, 1)]
        else:
            blocks = [self.src.at[self.rows(2 * j + 1 - p.core)] for j in (0, 1)]
        self.c1 = [self.go(blocks[j], self.r1.at[j], p.sib()) for j in (0, 1)]

    def two(self):
        p = self.p
        for copy in self.c1:
            copy.wait_recv()
        if self.src is None:

            @pl.loop(0, 2)
            def _(j):
                for c0, c1 in self.tiles():
                    self.r1[j, :, c0:c1] = (
                        self.product(2 * j + p.core, c0, c1) + self.r1[j, :, c0:c1].astype(F32)
                    ).astype(BF)

        else:

            @pl.loop(0, 18)
            def _(i):
                at = pl.ds(pl.multiple_of(i * 16, 16), 16)
                for j in (0, 1):
                    row = pl.multiple_of((2 * j + p.core) * 288 + i * 16, 16)
                    own = self.src[pl.ds(row, 16), :]
                    self.r1[j, at, :] = (own.astype(F32) + self.r1[j, at, :].astype(F32)).astype(BF)

        far = 1 - p.ylo
        self.c2 = [
            self.go(self.r1.at[far, pl.ds(0, 144)], self.r2.at[pl.ds(0, 144)], p.dy(1)),
            self.go(self.r1.at[far, pl.ds(144, 144)], self.r2.at[pl.ds(144, 144)], p.dy(3)),
        ]

    def three(self):
        p, cut = self.p, self.cut
        for copy in self.c2:
            copy.wait_recv()
        rest = self.n - cut

        @pl.loop(0, 9)
        def _(i):
            for h in (0, 1):
                at = pl.ds(pl.multiple_of(h * 144 + i * 16, 16), 16)
                to = pl.ds(pl.multiple_of(i * 16, 16), 16)
                total = (self.r1[p.ylo, at, :].astype(F32) + self.r2[at, :].astype(F32)).astype(BF)
                self.q[2 * h, to, :] = total[:, :cut]
                if rest == cut:
                    self.q[2 * h + 1, to, :] = total[:, cut:]
                else:
                    self.q[2 * h + 1, to, :] = jnp.concatenate(
                        [total[:, cut:], jnp.zeros((16, cut - rest), BF)], axis=1
                    )

        self.c3 = [
            self.go(self.q.at[(p.x + d) % 4], self.r3.at[d - 1], p.dx(d)) for d in (2, 1, 3)
        ]

    def four(self):
        p = self.p
        for copy in self.c3:
            copy.wait_recv()

        @pl.loop(0, 9)
        def _(i):
            at = pl.ds(pl.multiple_of(i * 16, 16), 16)
            total = self.q[p.x, at, :].astype(F32)
            for d in range(3):
                total = total + self.r3[d, at, :].astype(F32)
            self.r5[0, at, :] = total.astype(BF)

        self.c4 = self.go(self.r5.at[0], self.r4, p.dy(2))

    def five(self):
        p = self.p
        self.c4.wait()

        @pl.loop(0, 9)
        def _(i):
            at = pl.ds(pl.multiple_of(i * 16, 16), 16)
            self.r4[at, :] = (self.r5[0, at, :].astype(F32) + self.r4[at, :].astype(F32)).astype(BF)

        self.c5 = [self.go(self.r4, self.r5.at[d], p.dx(d)) for d in (2, 1, 3)]

    def six(self):
        p, cut = self.p, self.cut
        rest = self.n - cut
        for copy in self.c3:
            copy.wait_send()
        for copy in self.c5:
            copy.wait_recv()
        for d in range(4):
            held = self.r4 if d == 0 else self.r5.at[d]
            quarter = (p.x + 4 - d) % 4

            @pl.loop(0, 9)
            def _(i):
                at = pl.ds(pl.multiple_of(i * 16, 16), 16)
                self.q[quarter, at, :] = held[at, :]

        @pl.loop(0, 9)
        def _(i):
            at = pl.ds(pl.multiple_of(i * 16, 16), 16)
            for h in (0, 1):
                to = pl.ds(pl.multiple_of(h * 144 + i * 16, 16), 16)
                self.out[to, :cut] = self.q[2 * h, at, :].astype(F32)
                self.out[to, cut:] = self.q[2 * h + 1, at, :rest].astype(F32)

        for copy in self.c2 + self.c5:
            copy.wait_send()


def reduce_buffers(n, cut, computed):
    bufs = [
        pltpu.VMEM((2, 288, n), BF),
        pltpu.VMEM((288, n), BF),
        pltpu.VMEM((4, 144, cut), BF),
        pltpu.VMEM((3, 144, cut), BF),
        pltpu.VMEM((144, cut), BF),
        pltpu.VMEM((4, 144, cut), BF),
    ] + sems(12)
    return [pltpu.VMEM((2, 288, n), BF)] + bufs if computed else bufs


def norm_back(v, gain, dy):
    r = lax.rsqrt(jnp.mean(v * v, axis=-1, keepdims=True) + EPS)
    gdy = gain * dy
    dv = r * gdy - v * (r * r * r * jnp.mean(gdy * v, axis=-1, keepdims=True))
    return dv, r * v * dy


def turn_back(d, cosine, sine):
    d1, d2 = d[:, :128], d[:, 128:]
    return jnp.concatenate([d1 * cosine + d2 * sine, d2 * cosine - d1 * sine], axis=1)


BACK_IN = (
    "x",
    "d_ffn_t",
    "hidden",
    "normed2_t",
    "d_gate",
    "d_up",
    "middle",
    "branch",
    "cot",
    "tokens",
    "gains",
    "dg3",
    "attn",
    "attn_low",
    "lse",
    "queries",
    "kv",
    "key_pos",
    "query_pos",
    "small",
    "normed_t",
    "q_proj",
    "k_proj",
    "heads",
    "cosine",
    "sine",
)
BACK_OUT = (
    "grad_tokens",
    "o_down",
    "o_gate",
    "o_up",
    "o_oq",
    "o_kv",
)


def back_kernel(*refs):
    n_in, n_out = len(BACK_IN), len(BACK_OUT)
    i = dict(zip(BACK_IN, refs))
    o = dict(zip(BACK_OUT, refs[n_in:]))
    rest = list(refs[n_in + n_out :])

    def take(n):
        got = rest[:n]
        del rest[:n]
        return got

    p = Place()
    scale = HD ** (-0.5)
    z1 = take(6)
    z2 = take(6)
    (extra, xgot, d_mid, d_branch, d_attn, delta, dq, parts, got) = take(9)
    (kv_low, dn_kv, acc, gt, hg, oq, tail) = take(7)
    ks, kr, ks2, kr2, xs, xr = take(6)
    down = Reduce(p, o["o_down"], take(9), 896, left=i["d_ffn_t"], right=i["hidden"])
    gate = Reduce(p, o["o_gate"], take(9), 896, left=i["normed2_t"], right=i["d_gate"])
    up = Reduce(p, o["o_up"], [down.sent] + take(8), 896, left=i["normed2_t"], right=i["d_up"])
    roq = Reduce(p, o["o_oq"], take(8), 256, src=oq)
    rkv = Reduce(p, o["o_kv"], take(8), 384, src=tail)
    first = ZSum(p, i["x"], *z1)
    x2 = first.out
    second = ZSum(p, x2, *z2)
    wq, wk, wv, wo = [slice(256 * j, 256 * j + 256) for j in range(4)]
    small = i["small"]

    greet([p.sib(), p.dy(1), p.dy(3)] + [p.dcz(d) for d in range(1, 32)])
    first.start()
    down.one()
    first.middle()
    gate.one()
    down.two()
    acc[...] = jnp.zeros_like(acc)
    gt[...] = jnp.zeros_like(gt)
    hg[...] = jnp.zeros_like(hg)
    extra[...] = jnp.zeros_like(extra)
    first.finish()

    @pl.loop(0, 16)
    def _(b):
        at = pl.ds(pl.multiple_of(b * 16, 16), 16)
        dm, dg = norm_back(
            i["middle"][at, :], i["gains"][2:3, :], first.out[at, :].astype(F32)
        )
        acc[2] += dg
        dm = dm + i["cot"][at, :].astype(F32)
        d_mid[at, :] = dm
        db, dg = norm_back(i["branch"][at, :].astype(F32), i["gains"][1:2, :], dm)
        acc[1] += dg
        d_branch[at, :] = db.astype(BF)

    d_attn[...] = plain(d_branch[...], small[:, wo]).astype(BF)
    delta[...] = jnp.sum(d_attn[...].astype(F32) * i["attn"][...], axis=-1, keepdims=True)
    dq[...] = jnp.zeros_like(dq)

    def keys_block(kb):
        k, v = i["kv"][kb, :, :HD], i["kv"][kb, :, HD:]
        scores = against(i["queries"][...], k) * scale
        seen = i["key_pos"][kb] <= i["query_pos"][...]
        probs = jnp.where(seen, jnp.exp(scores - i["lse"][...]), 0.0)
        d_probs = against(d_attn[...], v)
        ds = (probs * (d_probs - delta[...])).astype(BF)
        dq[...] += plain(ds, k)
        dk = inner(ds, i["queries"][...]) * scale
        dv = inner(probs.astype(BF), d_attn[...])
        parts[kb, :, :HD] = dk.astype(BF)
        parts[kb, :, HD:] = dv.astype(BF)

    def kv_copy(kb, d, dz, device):
        slot = (d % 8) * 4 + dz
        row = pl.ds(pl.multiple_of(((p.z + dz) % 4) * 64, 64), 64)
        return pltpu.make_async_remote_copy(
            src_ref=parts.at[kb, row],
            dst_ref=got.at[slot],
            send_sem=ks.at[slot],
            recv_sem=kr.at[slot],
            device_id=device,
            device_id_type=MESH,
        )

    @pl.loop(1, 8)
    def _(d):
        kb = (p.c + d) % 8
        keys_block(kb)
        for dz in range(4):
            kv_copy(kb, d, dz, (p.f, kb, (p.z + dz) % 4)).start()

    keys_block(p.c)
    for dz in range(1, 4):
        kv_copy(p.c, 8, dz, p.dz(dz)).start()

    @pl.loop(0, 4)
    def _(b):
        at = pl.ds(pl.multiple_of(b * 64, 64), 64)
        dn = turn_back(dq[at, :] * scale, i["cosine"][at, :], i["sine"][at, :])
        dv, dg = norm_back(i["q_proj"][at, :], i["heads"][4:5, :], dn)
        acc[3, :, :HD] += dg.reshape(4, 16, HD).sum(axis=0)
        dq[at, :] = dv

    dq_low = dq[...].astype(BF)
    x2[...] = against(dq_low, small[:, wq]).astype(BF)
    extra[0:1, :] = jnp.sum(acc[3, :, :HD], axis=0, keepdims=True).astype(BF)
    second.start()
    more = [
        send(extra, xgot.at[d - 1], xs.at[d - 1], xr.at[d - 1], p.dz(d)) for d in (1, 2, 3)
    ]
    gate.two()
    oq[:, :HD] = plain(i["normed_t"][...], dq_low).astype(BF)
    oq[:, HD:] = inner(d_branch[...], i["attn_low"][...]).astype(BF)
    roq.one()
    for copy in down.c1:
        copy.wait_send()
    up.one()
    down.three()
    second.middle()

    for slot in range(1, 32):
        d, dz = slot // 4, slot % 4
        kv_copy(p.c, d, dz, p.dcz(slot)).wait_recv()
    own = pl.ds(pl.multiple_of(p.z * 64, 64), 64)

    @pl.loop(0, 4)
    def _(b):
        at = pl.ds(pl.multiple_of(p.z * 64 + b * 16, 16), 16)
        to = pl.ds(pl.multiple_of(b * 16, 16), 16)
        total = parts[p.c, at, :].astype(F32)
        for slot in range(1, 32):
            total = total + got[slot, to, :].astype(F32)
        kv_low[at, :] = total.astype(BF)

    kv2 = [
        send(kv_low.at[own], kv_low.at[own], ks2.at[d - 1], kr2.at[d - 1], p.dz(d))
        for d in (2, 1, 3)
    ]
    up.two()
    gate.three()
    down.four()
    for copy in kv2:
        copy.wait_recv()
    acc[3] = jnp.zeros_like(acc[3])

    @pl.loop(0, 4)
    def _(b):
        at = pl.ds(pl.multiple_of(b * 64, 64), 64)
        dn = turn_back(kv_low[at, :HD].astype(F32), i["cosine"][at, :], i["sine"][at, :])
        dv, dg = norm_back(i["k_proj"][at, :], i["heads"][5:6, :], dn)
        acc[3, :, :HD] += dg.reshape(4, 16, HD).sum(axis=0)
        dq[at, :] = dv

    dk_low = dq[...].astype(BF)
    dn_kv[...] = against(dk_low, small[:, wk]) + against(kv_low[:, HD:], small[:, wv])
    tail[:, :HD] = plain(i["normed_t"][...], dk_low).astype(BF)
    tail[:, HD : 2 * HD] = plain(i["normed_t"][...], kv_low[:, HD:]).astype(BF)
    for copy in more:
        copy.wait()
    heads = extra[0:1, :].astype(F32)
    for d in range(3):
        heads = heads + xgot[d, 0:1, :].astype(F32)
    hg[4:5, :] = heads
    hg[5:6, :] = jnp.sum(acc[3, :, :HD], axis=0, keepdims=True)
    second.finish()

    @pl.loop(0, 16)
    def _(b):
        at = pl.ds(pl.multiple_of(b * 16, 16), 16)
        dn = second.out[at, :].astype(F32) + dn_kv[at, :]
        dv, dg = norm_back(i["tokens"][at, :].astype(F32), i["gains"][0:1, :], dn)
        acc[0] += dg
        o["grad_tokens"][at, :] = d_mid[at, :] + dv

    for g in range(3):
        gt[g : g + 1, :] = jnp.sum(acc[g], axis=0, keepdims=True)
    gt[3:4, :] = i["dg3"][...]
    last = gt[...].T
    heads_t = hg[...].T
    tail[:, 2 * HD :] = last.astype(BF)
    for f in range(4):
        tail[288 * f : 288 * f + 64, 2 * HD :] = (
            last[288 * f : 288 * f + 64] + heads_t[64 * f : 64 * f + 64]
        ).astype(BF)
    rkv.one()
    roq.two()
    rkv.two()
    down.five()
    up.three()
    gate.four()
    roq.three()
    rkv.three()
    gate.five()
    up.four()
    roq.four()
    rkv.four()
    down.six()
    up.five()
    roq.five()
    rkv.five()
    gate.six()
    up.six()
    roq.six()
    rkv.six()
    for slot in range(1, 32):
        kv_copy(p.c, slot // 4, slot % 4, p.dcz(slot)).wait_send()
    for copy in kv2 + gate.c1 + up.c1 + roq.c1 + rkv.c1:
        copy.wait_send()


def back_call(ins, cid):
    def zsum():
        return [pltpu.VMEM((3, 64, 1152), BF), pltpu.VMEM((256, 1152), BF)] + sems(3) + sems(3)

    scratch = (
        zsum()
        + zsum()
        + [
            pltpu.VMEM((16, HD), BF),
            pltpu.VMEM((3, 16, HD), BF),
            pltpu.VMEM((256, 1152), F32),
            pltpu.VMEM((256, 1152), BF),
            pltpu.VMEM((256, HD), BF),
            pltpu.VMEM((256, 1), F32),
            pltpu.VMEM((256, HD), F32),
            pltpu.VMEM((8, 256, 2 * HD), BF),
            pltpu.VMEM((32, 64, 2 * HD), BF),
            pltpu.VMEM((256, 2 * HD), BF),
            pltpu.VMEM((256, 1152), F32),
            pltpu.VMEM((4, 16, 1152), F32),
            pltpu.VMEM((128, 1152), F32),
            pltpu.VMEM((128, HD), F32),
            pltpu.VMEM((1152, 512), BF),
            pltpu.VMEM((1152, 640), BF),
        ]
        + sems(32)
        + sems(3)
        + sems(3)
        + reduce_buffers(1728, 896, True) * 2
        + reduce_buffers(1728, 896, False)
        + reduce_buffers(512, 256, False)
        + reduce_buffers(640, 384, False)
    )
    shapes = [(256, 1152)] + [(288, n) for n in (1728, 1728, 1728, 512, 640)]
    return pl.pallas_call(
        back_kernel,
        out_shape=[jax.ShapeDtypeStruct(s, F32) for s in shapes],
        in_specs=[VM] * len(BACK_IN),
        out_specs=[VM] * len(shapes),
        scratch_shapes=scratch,
        compiler_params=params(cid, 62),
        name="backward",
    )(*[ins[name] for name in BACK_IN])


FORE_IN = (
    "tokens",
    "cot",
    "small",
    "w_gate",
    "w_up",
    "w_down",
    "cosine",
    "sine",
    "key_pos",
    "query_pos",
)
FORE_OUT = (
    "out",
    "small",
    "gains",
    "heads",
    "x",
    "d_ffn_t",
    "hidden",
    "normed2_t",
    "d_gate",
    "d_up",
    "middle",
    "branch",
    "dg3",
    "attn",
    "attn_low",
    "lse",
    "queries",
    "kv",
    "normed_t",
    "q_proj",
    "k_proj",
)
TILES = [(c0, min(c0 + 256, 1728)) for c0 in range(0, 1728, 256)]


def turn(v, cosine, sine):
    v1, v2 = v[:, :128], v[:, 128:]
    return jnp.concatenate([v1 * cosine - v2 * sine, v2 * cosine + v1 * sine], axis=1)


def transpose_into(dst, src):
    for c0 in range(0, 1152, 128):
        dst[c0 : c0 + 128, :] = src[:, c0 : c0 + 128].astype(F32).T.astype(BF)


def fore_kernel(*refs):
    n_in, n_out = len(FORE_IN), len(FORE_OUT)
    i = dict(zip(FORE_IN, refs))
    o = dict(zip(FORE_OUT, refs[n_in:]))
    rest = list(refs[n_in + n_out :])

    def take(n):
        got = rest[:n]
        del rest[:n]
        return got

    p = Place()
    scale = HD ** (-0.5)
    w_gate, w_up, w_down, act, slope, normed, d_ffn, probs, head_cols, accg = take(10)
    local, gs, gr, ks, kr, vs, vr, fs, fr = take(9)
    z1, z2 = take(6), take(6)
    part = take(1)[0]
    small = o["small"]
    first = ZSum(p, part, *z1)
    second = ZSum(p, part, *z2)
    kv = o["kv"]
    gathers = [
        Gather(p, src, dst, local.at[j], gs, gr, 4 * j)
        for j, (src, dst) in enumerate(
            [(i["small"], small), (i["w_gate"], w_gate), (i["w_up"], w_up), (i["w_down"], w_down)]
        )
    ]
    g_small, g_gate, g_up, g_down = gathers

    greet([p.sib(), p.dy(1), p.dy(3)] + [p.dc(d) for d in range(1, 8)] + [p.dz(d) for d in (1, 2, 3)])
    g_small.start()
    g_small.start_far()
    g_gate.start()
    g_up.start()
    g_down.start()
    accg[...] = jnp.zeros_like(accg)
    g_small.forward()
    g_gate.start_far()
    g_small.finish()

    o["gains"][...] = small[:, 1024:].astype(F32).T[:8, :]
    for f in range(4):
        head_cols[64 * f : 64 * f + 64, :] = small[288 * f : 288 * f + 64, 1024:].astype(F32)
    o["heads"][...] = head_cols[...].T[:8, :]

    @pl.loop(0, 16)
    def _(b):
        at = pl.ds(pl.multiple_of(b * 16, 16), 16)
        normed[at, :] = normalize(i["tokens"][at, :].astype(F32), o["gains"][0:1, :]).astype(BF)

    o["q_proj"][...] = plain(normed[...], small[:, :256])
    o["k_proj"][...] = plain(normed[...], small[:, 256:512])
    kv[p.c, :, HD:] = plain(normed[...], small[:, 512:768]).astype(BF)

    quarter = pl.ds(pl.multiple_of(p.z * 64, 64), 64)
    sent = [
        send(
            kv.at[p.c, quarter, pl.ds(HD, HD)],
            kv.at[p.c, quarter, pl.ds(HD, HD)],
            vs.at[d - 1],
            vr.at[d - 1],
            p.dc(d),
        )
        for d in range(1, 8)
    ]

    @pl.loop(0, 4)
    def _(b):
        at = pl.ds(pl.multiple_of(b * 64, 64), 64)
        n = normalize(o["k_proj"][at, :], o["heads"][5:6, :])
        kv[p.c, at, :HD] = turn(n, i["cosine"][at, :], i["sine"][at, :]).astype(BF)

    keys = kv.at[p.c, :, pl.ds(0, HD)]
    sent_k = [send(keys, keys, ks.at[d - 1], kr.at[d - 1], p.dc(d)) for d in range(1, 8)]

    @pl.loop(0, 4)
    def _(b):
        at = pl.ds(pl.multiple_of(b * 64, 64), 64)
        n = normalize(o["q_proj"][at, :], o["heads"][4:5, :])
        o["queries"][at, :] = turn(n, i["cosine"][at, :], i["sine"][at, :]).astype(BF)

    for copy in sent:
        copy.wait_recv()
    sent_z = []
    for d in range(8):
        block = kv.at[(p.c + 8 - d) % 8, quarter, pl.ds(HD, HD)]
        if d == 0:
            continue
        sent_z += [
            send(block, block, fs.at[3 * d + e - 1], fr.at[3 * d + e - 1], p.dz(e))
            for e in (2, 1, 3)
        ]
    transpose_into(o["normed_t"], normed)
    for copy in sent_k:
        copy.wait_recv()
    g_gate.forward()
    g_up.start_far()

    @pl.loop(0, 4)
    def _(b):
        at = pl.ds(pl.multiple_of(b * 64, 64), 64)
        query = o["queries"][at, :]
        seen = [i["key_pos"][kb] <= i["query_pos"][at, :] for kb in range(8)]
        scores = [against(query, kv[kb, :, :HD]) * scale for kb in range(8)]
        top = jnp.max(jnp.where(seen[0], scores[0], -1e30), axis=-1, keepdims=True)
        for kb in range(1, 8):
            top = jnp.maximum(
                top, jnp.max(jnp.where(seen[kb], scores[kb], -1e30), axis=-1, keepdims=True)
            )
        scores = [jnp.where(seen[kb], jnp.exp(scores[kb] - top), 0.0) for kb in range(8)]
        total = jnp.sum(scores[0], axis=-1, keepdims=True)
        for kb in range(1, 8):
            total = total + jnp.sum(scores[kb], axis=-1, keepdims=True)
        o["lse"][at, :] = top + jnp.log(total)
        share = 1.0 / total
        for kb in range(8):
            probs[kb, at, :] = (scores[kb] * share).astype(BF)

    for copy in sent_z:
        copy.wait_recv()
    attn = plain(probs[0], kv[0, :, HD:])
    for kb in range(1, 8):
        attn = attn + plain(probs[kb], kv[kb, :, HD:])
    o["attn"][...] = attn
    attn_low = attn.astype(BF)
    o["attn_low"][...] = attn_low
    part[...] = against(attn_low, small[:, 768:1024]).astype(BF)
    first.start()
    g_up.forward()
    g_down.start_far()
    first.middle()
    g_gate.finish()
    first.finish()

    @pl.loop(0, 16)
    def _(b):
        at = pl.ds(pl.multiple_of(b * 16, 16), 16)
        branch = first.out[at, :]
        o["branch"][at, :] = branch
        middle = i["tokens"][at, :].astype(F32) + normalize(
            branch.astype(F32), o["gains"][1:2, :]
        )
        o["middle"][at, :] = middle
        normed[at, :] = normalize(middle, o["gains"][2:3, :]).astype(BF)

    g_up.finish()
    for c0, c1 in TILES:
        gate = plain(normed[...], w_gate[:, c0:c1])
        up = plain(normed[...], w_up[:, c0:c1])
        bend = jnp.tanh(0.7978845608028654 * (gate + 0.044715 * gate * gate * gate))
        gelu = 0.5 * gate * (1.0 + bend)
        o["hidden"][:, c0:c1] = (gelu * up).astype(BF)
        act[:, c0:c1] = gelu
        rise = 0.7978845608028654 * (1.0 + 0.134145 * gate * gate)
        slope[:, c0:c1] = up * (0.5 * (1.0 + bend) + 0.5 * gate * (1.0 - bend * bend) * rise)
    g_down.forward()
    g_down.finish()
    for c0 in range(0, 1152, 384):
        part[:, c0 : c0 + 384] = against(o["hidden"][...], w_down[c0 : c0 + 384, :]).astype(BF)
    second.start()
    transpose_into(o["normed2_t"], normed)
    second.middle()
    second.finish()

    @pl.loop(0, 16)
    def _(b):
        at = pl.ds(pl.multiple_of(b * 16, 16), 16)
        ffn = second.out[at, :].astype(F32)
        o["out"][at, :] = (o["middle"][at, :] + normalize(ffn, o["gains"][3:4, :])).astype(BF)
        dv, dg = norm_back(ffn, o["gains"][3:4, :], i["cot"][at, :].astype(F32))
        accg[...] += dg
        d_ffn[at, :] = dv.astype(BF)

    o["dg3"][...] = jnp.sum(accg[...], axis=0, keepdims=True)
    transpose_into(o["d_ffn_t"], d_ffn)
    for c0, c1 in TILES:
        d_hidden = plain(d_ffn[...], w_down[:, c0:c1])
        o["d_up"][:, c0:c1] = (d_hidden * act[:, c0:c1]).astype(BF)
        o["d_gate"][:, c0:c1] = (d_hidden * slope[:, c0:c1]).astype(BF)
    for c0 in range(0, 1152, 384):
        o["x"][:, c0 : c0 + 384] = (
            against(o["d_gate"][...], w_gate[c0 : c0 + 384, :])
            + against(o["d_up"][...], w_up[c0 : c0 + 384, :])
        ).astype(BF)
    for copy in sent + sent_k + sent_z:
        copy.wait_send()


def fore_call(ins, cid):
    def zsum():
        return [pltpu.VMEM((3, 64, 1152), BF), pltpu.VMEM((256, 1152), BF)] + sems(3) + sems(3)

    scratch = (
        [pltpu.VMEM((1152, 1728), BF)] * 3
        + [
            pltpu.VMEM((256, 1728), F32),
            pltpu.VMEM((256, 1728), F32),
            pltpu.VMEM((256, 1152), BF),
            pltpu.VMEM((256, 1152), BF),
            pltpu.VMEM((8, 256, 256), BF),
            pltpu.VMEM((256, 128), F32),
            pltpu.VMEM((16, 1152), F32),
            pltpu.SemaphoreType.DMA((4,)),
        ]
        + sems(16)
        + sems(7)
        + sems(7)
        + sems(24)
        + zsum()
        + zsum()
        + [pltpu.VMEM((256, 1152), BF)]
    )
    shapes = dict(
        out=((256, 1152), BF),
        small=((1152, 1152), BF),
        gains=((8, 1152), F32),
        heads=((8, 256), F32),
        x=((256, 1152), BF),
        d_ffn_t=((1152, 256), BF),
        hidden=((256, 1728), BF),
        normed2_t=((1152, 256), BF),
        d_gate=((256, 1728), BF),
        d_up=((256, 1728), BF),
        middle=((256, 1152), F32),
        branch=((256, 1152), BF),
        dg3=((1, 1152), F32),
        attn=((256, 256), F32),
        attn_low=((256, 256), BF),
        lse=((256, 1), F32),
        queries=((256, 256), BF),
        kv=((8, 256, 512), BF),
        normed_t=((1152, 256), BF),
        q_proj=((256, 256), F32),
        k_proj=((256, 256), F32),
    )
    done = pl.pallas_call(
        fore_kernel,
        out_shape=[jax.ShapeDtypeStruct(*shapes[name]) for name in FORE_OUT],
        in_specs=[VM] * len(FORE_IN),
        out_specs=[VM] * len(FORE_OUT),
        scratch_shapes=scratch,
        compiler_params=params(cid, 62),
        name="forward",
    )(*[ins[name] for name in FORE_IN])
    return dict(zip(FORE_OUT, done))


def per_device(
    tokens,
    block_order,
    cotangent,
    w_query,
    w_key,
    w_value,
    w_out,
    w_gate,
    w_up,
    w_down,
    gains,
    head_gains,
):
    _, rows, width = tokens.shape
    cycle_index = lax.axis_index("context")
    span = rows // 2
    seq_len = rows * 8

    small = jnp.concatenate(
        [
            w_query,
            w_key,
            w_value,
            w_out.T,
            jnp.pad(
                jnp.concatenate(
                    [gains.T, jnp.pad(head_gains.T, ((0, 288 - 64), (0, 0)))], axis=1
                ),
                ((0, 0), (0, 122)),
            ),
        ],
        axis=1,
    )
    offsets = jnp.arange(seq_len, dtype=jnp.int32)
    key_pos = (jnp.repeat(block_order, span, axis=1) * span + (offsets % span)[None, :])[0]
    query_pos = lax.dynamic_slice_in_dim(key_pos, cycle_index * rows, rows, 0)
    cosine, sine = tables(query_pos)
    ins = dict(
        tokens=tokens[0],
        cot=cotangent[0],
        small=small,
        w_gate=w_gate,
        w_up=w_up,
        w_down=w_down.T,
        cosine=cosine,
        sine=sine,
        key_pos=key_pos.reshape(8, 1, rows),
        query_pos=query_pos[:, None],
    )
    held = fore_call(ins, 1)
    result = held["out"][None]
    grad_tokens, sum_down, sum_gate, sum_up, sum_oq, sum_kv = back_call({**ins, **held}, 2)
    return (
        result,
        grad_tokens[None],
        sum_oq[:, :HD],
        sum_kv[:, :HD],
        sum_kv[:, HD : 2 * HD],
        sum_oq[:, HD:].T,
        sum_gate,
        sum_up,
        sum_down.T,
        sum_kv[:, 512:516].T,
        sum_kv[:64, 516:518].T,
    )


def solution(mesh):
    in_specs = (
        P("fsdp", "context", None),
        P("fsdp", None),
        P("fsdp", "context", None),
        P("fsdp", "tensor"),
        P("fsdp", None),
        P("fsdp", None),
        P("tensor", "fsdp"),
        P("fsdp", "tensor"),
        P("fsdp", "tensor"),
        P("tensor", "fsdp"),
        P(None, "fsdp"),
        P(None, "fsdp"),
    )
    out_specs = (
        P("fsdp", "context", None),
        P("fsdp", "context", None),
        P("fsdp", "tensor"),
        P("fsdp", None),
        P("fsdp", None),
        P("tensor", "fsdp"),
        P("fsdp", "tensor"),
        P("fsdp", "tensor"),
        P("tensor", "fsdp"),
        P(None, "fsdp"),
        P(None, "fsdp"),
    )
    return jax.shard_map(
        per_device, mesh=mesh, in_specs=in_specs, out_specs=out_specs, check_vma=False
    )
```

time: 1010 us -> 290 us (0.29)
  waiting for transfers between devices: 801 us -> 0 us
  Pallas kernels: 0 us -> 263 us
  blocking collectives: 79.1 us -> 0 us
  matrix products: 53.7 us -> 0 us
  other arithmetic: 39.7 us -> 3.26 us
  between operations: 16.9 us -> 0.72 us
    reduce_scatter x8 -> x0, waiting for transfers between devices: 354 us -> none  [the longest x1 187 us: per_device(): lax.psum_scatter(jnp.concatenate([d_key_part, d_value_part], axis=1).asty...]
    pallas_call x0 -> x2, Pallas kernels: none -> 263 us  [the longest x1 153 us: back_call(): pl.pallas_call(back_kernel, out_shape=[jax.ShapeDtypeStruct(s, F32) for s...]
    psum x5 -> x0, waiting for transfers between devices: 225 us -> none  [the longest x1 62.5 us: per_device(): lax.psum(owned[0].astype(jnp.bfloat16), 'context').astype(jnp.float32)]
    all_gather x5 -> x0, waiting for transfers between devices: 147 us -> none  [the longest x1 46 us: per_device(): lax.all_gather(values, 'context', axis=0, tiled=True)]
    unnamed x22 -> x0, waiting for transfers between devices: 74.5 us -> none
    dot_general x27 -> x0, matrix products: 53.7 us -> none  [the longest x7 19.6 us: plain(): return jnp.dot(left, right, preferred_element_type=jnp.float32)]
    all_gather x6 -> x0, blocking collectives: 43.1 us -> none  [the longest x1 9.04 us: per_device(): lax.all_gather(w_query, 'fsdp', axis=0, tiled=True)]
    psum x2 -> x0, blocking collectives: 36 us -> none  [the longest x1 25.3 us: per_device(): lax.psum(owned[7].astype(jnp.bfloat16), 'context').astype(jnp.float32)]
  transfers between devices with their start and end apart: 20 -> 0, of which waited for: 17 -> 0; matrix products, arithmetic and copies ran while one was open for 5% -> 0% of each run, Pallas kernels for 0% -> 0%
where the time goes in v1:
time: 290 us; the launch traced here: 288 us
  Pallas kernels  263 us (91%)
  local copies, waits for them, and re-layouts  20.1 us (7%)
  other arithmetic  3.26 us (1%)
    pallas_call x1, Pallas kernels, back_call(): pl.pallas_call(back_kernel, out_shape=[jax.ShapeDtypeStruct(s, F32) for s...  153 us
    pallas_call x1, Pallas kernels, fore_call(): pl.pallas_call(fore_kernel, out_shape=[jax.ShapeDtypeStruct(*shapes[name]...  111 us
    unnamed x21, local copies, waits for them, and re-layouts  14.8 us

profile of v1, /device:TPU:0, one launch (start us, length us, event | category | flops | bytes accessed | tf_op | source)
XLA Modules:
  0.0 287.5 jit_solution(2342673364745862795)
XLA Ops:
  0.7 0.7 multiply_reduce_fusion
  1.5 0.6 fusion.1.refs_8_.refs_17_
  2.1 0.7 fusion.3
  3.0 0.8 copy.34.refs_9_.refs_18_
  3.9 1.2 multiply_sine_fusion
  5.1 0.9 constant_dynamic-update-slice_fusion.2
  6.0 0.9 constant_dynamic-update-slice_fusion.1
  6.9 0.9 constant_dynamic-update-slice_fusion
  7.9 0.9 bitcast_dynamic-update-slice_fusion
  8.8 0.8 copy-done.4
  9.7 110.8 %forward.1 = (bf16[256,1152]{1,0:T(8,128)(2,1)}, bf16[1152,1152]{1,0:T(8,128)(2,1)}, f32[8,1152]{1,0:T(8,128)}, f32[8,256]{1,0:T(8,128)}, bf16[256,1152]{1,0:T(8...) custom-call(bf16[256,1152]{1,0:T(8,128)(2,1)} %bitcast.22, ...), custom_call_target="tpu_custom_call" | custom-call | tf_op jit(solution)/shard_map/forward/pallas_call | solution.py:951
  120.4 152.7 %backward.1 = (f32[256,1152]{1,0:T(8,128)}, f32[288,1728]{1,0:T(8,128)}, f32[288,1728]{1,0:T(8,128)}, f32[288,1728]{1,0:T(8,128)}, f32[288,512]{1,0:T(8,128)}, /*index=5*/f32[288,640]{1,0:T(8,128)}) custom-call(bf16[256,1152]{1,0:T(8,128)(2,1)} %get-tuple-element.39.refs_0_, bf16[1152,256]{1,0:T(8,128)(2,1)} %get-tuple-element.40.refs_1_, ...), custom_call_target="tpu_custom_call" | custom-call | tf_op jit(solution)/shard_map/backward/pallas_call | solution.py:657
  273.2 0.9 slice_bitcast_fusion.2
  274.1 0.6 copy.37
  274.7 0.9 slice_bitcast_fusion.1
  275.6 2.3 slice_bitcast_fusion
  277.9 0.7 copy.36
  278.6 1.9 copy.47
  280.5 1.0 copy.48
  281.6 1.3 copy.49
  282.9 1.0 copy-done.1
  283.9 1.3 copy.50
  285.2 1.0 copy-done
  286.2 1.3 copy.51
  (14 shorter events, 0.4 us)
Async XLA Ops:
  8.8 0.8 copy-start.4
  273.1 7.4 %copy-start.3 = (f32[256,1152]{1,0:T(8,128)S(1)}, f32[256,1152]{1,0:T(8,128)}, u32[]{:S(2)}) copy-start(f32[256,1152]{1,0:T(8,128)} %get-tuple-element.59) | copy-start | bytes 3538948
  277.9 3.6 %copy-start.2 = (f32[288,1728]{1,0:T(8,128)S(1)}, f32[288,1728]{1,0:T(8,128)}, u32[]{:S(2)}) copy-start(f32[288,1728]{1,0:T(8,128)} %get-tuple-element.127) | copy-start | bytes 5971972
  281.6 2.3 copy-start.1
  283.9 2.3 copy-start

commit v2 on v1

v2 whole, which is shorter than its diff:
```python
import functools
import math
from typing import Any, NamedTuple

import jax
import jax.numpy as jnp
from jax import lax
from jax.experimental import pallas as pl
from jax.experimental.pallas import tpu as pltpu
from jax.sharding import PartitionSpec as P

HD = 256
ROPE_BASE = 1000000.0
EPS = 1e-06
MESH = pl.DeviceIdType.MESH
BF = jnp.bfloat16
F32 = jnp.float32


def normalize(values, gain):
    return values * lax.rsqrt(jnp.mean(values * values, axis=-1, keepdims=True) + EPS) * gain


def rotate(values, cosine, sine):
    middle = values.shape[-1] // 2
    first = values[..., :middle]
    second = values[..., middle:]
    return jnp.concatenate(
        [first * cosine - second * sine, second * cosine + first * sine], axis=-1
    )


def tables(positions):
    steps = jnp.arange(HD // 2, dtype=jnp.float32) * (2.0 / HD)
    inverse = jnp.exp(-math.log(ROPE_BASE) * steps)
    angle = positions.astype(jnp.float32)[:, None] * inverse[None, :]
    return (jnp.cos(angle), jnp.sin(angle))


def plain(left, right):
    return jnp.dot(left, right, preferred_element_type=jnp.float32)


def inner(left, right):
    return lax.dot_general(
        left, right, (((0,), (0,)), ((), ())), preferred_element_type=jnp.float32
    )


def against(left, right):
    return lax.dot_general(
        left, right, (((1,), (1,)), ((), ())), preferred_element_type=jnp.float32
    )


class Place:
    def __init__(self):
        f = lax.axis_index("fsdp")
        c = lax.axis_index("context")
        self.f, self.c, self.z = f, c, lax.axis_index("tensor")
        self.ylo, self.core = f // 2, f % 2
        self.x, self.yhi = c // 2, c % 2
        self.y = self.yhi * 2 + self.ylo

    def at(self, x=None, y=None, z=None, core=None):
        x = self.x if x is None else x
        y = self.y if y is None else y
        z = self.z if z is None else z
        core = self.core if core is None else core
        return ((y % 2) * 2 + core, x * 2 + y // 2, z)

    def sib(self):
        return self.at(core=1 - self.core)

    def dy(self, d):
        return self.at(y=(self.y + d) % 4)

    def dx(self, d):
        return self.at(x=(self.x + d) % 4)

    def dz(self, d):
        return self.at(z=(self.z + d) % 4)

    def dc(self, d):
        return (self.f, (self.c + d) % 8, self.z)


def greet(devices):
    barrier = pltpu.get_barrier_semaphore()
    for device in devices:
        pl.semaphore_signal(barrier, inc=1, device_id=device, device_id_type=MESH)
    pl.semaphore_wait(barrier, len(devices))


def send(src, dst, ssem, rsem, device):
    copy = pltpu.make_async_remote_copy(
        src_ref=src, dst_ref=dst, send_sem=ssem, recv_sem=rsem, device_id=device, device_id_type=MESH
    )
    copy.start()
    return copy


def sems(n):
    return [pltpu.SemaphoreType.DMA((n,)), pltpu.SemaphoreType.DMA((n,))]


VM = pl.BlockSpec(memory_space=pltpu.VMEM)


def params(cid, limit=48):
    return pltpu.CompilerParams(
        collective_id=cid, has_side_effects=True, vmem_limit_bytes=limit * 2**20
    )


class Gather:
    def __init__(self, place, src, out, local, ssem, rsem, base, relay=False):
        self.p, self.src, self.out = place, src, out
        self.local, self.ssem, self.rsem, self.base = local, ssem, rsem, base
        self.rows, self.relay = src.shape[0], relay

    def go(self, n, src, dst, device):
        return send(src, dst, self.ssem.at[self.base + n], self.rsem.at[self.base + n], device)

    def at(self, row, n):
        return self.out.at[pl.ds(pl.multiple_of(row, 16), n)]

    def start(self):
        p, rows = self.p, self.rows
        own = self.at(p.f * rows, rows)
        self.s = self.go(2, self.src, own, p.sib())
        self.l = pltpu.make_async_copy(self.src, own, self.local)
        self.l.start()

    def start_far(self):
        p, rows, half = self.p, self.rows, self.rows // 2
        first, n = (64 * (p.x % 2), 80) if self.relay else (0, half)
        self.y = []
        for h, d in ((0, 1), (1, 3)):
            row = first + half * h
            src = self.src.at[pl.ds(pl.multiple_of(row, 16), n)]
            self.y.append(self.go(h, src, self.at(p.f * rows + row, n), p.dy(d)))

    def across(self):
        p, half = self.p, self.rows // 2
        for copy in self.y:
            copy.wait_recv()
        row = (2 * (1 - p.ylo) + p.core) * self.rows
        flip, back = p.x + 1 - 2 * (p.x % 2), 3 - p.x
        self.w = []
        for h, x in ((0, flip), (1, back)):
            part = self.at(row + half * h + 80 * (p.x % 2), 64)
            self.w.append(self.go(4 + h, part, part, p.at(x=x)))

    def forward(self):
        p, rows = self.p, self.rows
        for copy in self.w if self.relay else self.y:
            copy.wait_recv()
        block = self.at((2 * (1 - p.ylo) + p.core) * rows, rows)
        self.t = self.go(3, block, block, p.sib())

    def finish(self):
        self.l.wait()
        for copy in self.y:
            copy.wait_send()
        if self.relay:
            for copy in self.w:
                copy.wait_send()
        self.s.wait()
        self.t.wait()


class ZSum:
    def __init__(self, place, x, out, base, got, s1, r1, s2, r2):
        self.p, self.x, self.got, self.out = place, x, got, out
        self.base, self.share = base, got.shape[1]
        self.s1, self.r1, self.s2, self.r2 = s1, r1, s2, r2

    def rows(self, block):
        return pl.ds(pl.multiple_of(self.base + block * self.share, 32), self.share)

    def start(self):
        p = self.p
        self.c1 = [
            send(
                self.x.at[self.rows((p.z + d) % 4)],
                self.got.at[d - 1],
                self.s1.at[d - 1],
                self.r1.at[d - 1],
                p.dz(d),
            )
            for d in (2, 1, 3)
        ]

    def middle(self):
        p = self.p
        for copy in self.c1:
            copy.wait_recv()
        own = self.rows(p.z)

        @pl.loop(0, self.share // 16)
        def _(i):
            at = pl.ds(pl.multiple_of(self.base + p.z * self.share + i * 16, 16), 16)
            to = pl.ds(pl.multiple_of(i * 16, 16), 16)
            total = self.x[at, :].astype(F32)
            for d in range(3):
                total = total + self.got[d, to, :].astype(F32)
            self.out[at, :] = total.astype(BF)

        self.c2 = [
            send(self.out.at[own], self.out.at[own], self.s2.at[d - 1], self.r2.at[d - 1], p.dz(d))
            for d in (2, 1, 3)
        ]

    def finish(self):
        for copy in self.c1:
            copy.wait_send()
        for copy in self.c2:
            copy.wait()


class Reduce:
    def __init__(self, place, out, bufs, cut, src=None, left=None, right=None, direct=False):
        self.p, self.src, self.left, self.right = place, src, left, right
        self.outs, self.cut = out, cut
        if src is None:
            self.sent, bufs = bufs[0], bufs[1:]
        self.r1, self.r2, self.q, self.r3, self.r4, self.r5, self.r6, self.s, self.r = bufs
        self.n = sum(ref.shape[1] for ref in out)
        self.ns, self.direct = 0, direct
        x, side = place.x, (cut // 128 + 1) // 2 * 128
        flip, back = x + 1 - 2 * (x % 2), 3 - x
        self.ways = [
            (flip, back, 3 - flip, pl.ds(0, side)),
            (back, flip, back + 1 - 2 * (back % 2), pl.ds(side, cut - side)),
        ]

    def go(self, src, dst, device):
        i = self.ns
        self.ns += 1
        return send(src, dst, self.s.at[i], self.r.at[i], device)

    def rows(self, block):
        return pl.ds(pl.multiple_of(block * 288, 16), 288)

    def product(self, block, c0, c1):
        return plain(self.left[self.rows(block), :], self.right[:, c0:c1])

    def tiles(self):
        return [(c0, min(c0 + 256, self.n)) for c0 in range(0, self.n, 256)]

    def one(self):
        p = self.p
        if self.src is None:

            @pl.loop(0, 2)
            def _(j):
                for c0, c1 in self.tiles():
                    self.sent[j, :, c0:c1] = self.product(2 * j + 1 - p.core, c0, c1).astype(BF)

            blocks = [self.sent.at[j] for j in (0, 1)]
        else:
            blocks = [self.src.at[self.rows(2 * j + 1 - p.core)] for j in (0, 1)]
        self.c1 = [self.go(blocks[j], self.r1.at[j], p.sib()) for j in (0, 1)]

    def two(self):
        p = self.p
        for copy in self.c1:
            copy.wait_recv()
        if self.src is None:

            @pl.loop(0, 2)
            def _(j):
                for c0, c1 in self.tiles():
                    self.r1[j, :, c0:c1] = (
                        self.product(2 * j + p.core, c0, c1) + self.r1[j, :, c0:c1].astype(F32)
                    ).astype(BF)

        else:

            @pl.loop(0, 18)
            def _(i):
                at = pl.ds(pl.multiple_of(i * 16, 16), 16)
                for j in (0, 1):
                    row = pl.multiple_of((2 * j + p.core) * 288 + i * 16, 16)
                    own = self.src[pl.ds(row, 16), :]
                    self.r1[j, at, :] = (own.astype(F32) + self.r1[j, at, :].astype(F32)).astype(BF)

        far = 1 - p.ylo
        self.c2 = [
            self.go(self.r1.at[far, pl.ds(0, 144)], self.r2.at[pl.ds(0, 144)], p.dy(1)),
            self.go(self.r1.at[far, pl.ds(144, 144)], self.r2.at[pl.ds(144, 144)], p.dy(3)),
        ]

    def three(self):
        p, cut = self.p, self.cut
        for copy in self.c2:
            copy.wait_recv()
        rest = self.n - cut

        @pl.loop(0, 9)
        def _(i):
            for h in (0, 1):
                at = pl.ds(pl.multiple_of(h * 144 + i * 16, 16), 16)
                to = pl.ds(pl.multiple_of(i * 16, 16), 16)
                total = (self.r1[p.ylo, at, :].astype(F32) + self.r2[at, :].astype(F32)).astype(BF)
                self.q[2 * h, to, :] = total[:, :cut]
                if rest == cut:
                    self.q[2 * h + 1, to, :] = total[:, cut:]
                else:
                    self.q[2 * h + 1, to, :] = jnp.concatenate(
                        [total[:, cut:], jnp.zeros((16, cut - rest), BF)], axis=1
                    )

        if self.direct:
            self.c3 = [
                self.go(self.q.at[(p.x + d) % 4], self.r3.at[d - 1], p.dx(d)) for d in (2, 1, 3)
            ]
            return
        self.c3 = []
        for one, two, theirs, cols in self.ways:
            for k, quarter in enumerate((one, theirs)):
                self.c3.append(
                    self.go(self.q.at[quarter, :, cols], self.r3.at[k, :, cols], p.at(x=one))
                )

    def sum_rows(self, dst, first, *more):
        @pl.loop(0, 9)
        def _(i):
            at = pl.ds(pl.multiple_of(i * 16, 16), 16)
            total = first[at, :].astype(F32)
            for ref in more:
                total = total + ref[at, :].astype(F32)
            dst[at, :] = total.astype(BF)

    def four(self):
        p = self.p
        for copy in self.c3:
            copy.wait_recv()
        if self.direct:
            return
        mine = self.q.at[p.x]
        self.sum_rows(mine, mine, self.r3.at[0])
        self.c3b = []
        for one, two, _, cols in self.ways:
            held = self.q.at[two, :, cols]
            self.sum_rows(held, held, self.r3.at[1, :, cols])
            self.c3b.append(self.go(held, self.r3.at[2, :, cols], p.at(x=two)))

    def fourb(self):
        p = self.p
        if self.direct:
            self.sum_rows(self.r6, self.q.at[p.x], *[self.r3.at[d] for d in range(3)])
        else:
            for copy in self.c3b:
                copy.wait_recv()
            self.sum_rows(self.r6, self.q.at[p.x], self.r3.at[2])
        self.c4 = self.go(self.r6, self.r4, p.dy(2))

    def five(self):
        p = self.p
        self.c4.wait()
        mine = self.r5.at[p.x]
        self.sum_rows(mine, self.r6, self.r4)
        if self.direct:
            self.c5 = [self.go(mine, mine, p.dx(d)) for d in (2, 1, 3)]
            return
        self.c5 = []
        for one, two, _, cols in self.ways:
            part = self.r5.at[p.x, :, cols]
            self.c5.append(self.go(part, part, p.at(x=two)))
            self.c5.append(self.go(part, part, p.at(x=one)))

    def fiveb(self):
        p = self.p
        self.c5b = []
        if self.direct:
            return
        for k, (one, two, _, cols) in enumerate(self.ways):
            self.c5[2 * k].wait_recv()
            part = self.r5.at[two, :, cols]
            self.c5b.append(self.go(part, part, p.at(x=one)))

    def put(self, rows, c0, value):
        start = 0
        for ref in self.outs:
            end = start + ref.shape[1]
            lo, hi = max(c0, start), min(c0 + value.shape[1], end)
            if lo < hi:
                ref[rows, lo - start : hi - start] = value[:, lo - c0 : hi - c0]
            start = end

    def six(self):
        rest = self.n - self.cut
        for copy in self.c5b + (self.c5 if self.direct else self.c5[1::2]):
            copy.wait_recv()

        @pl.loop(0, 9)
        def _(i):
            at = pl.ds(pl.multiple_of(i * 16, 16), 16)
            for h in (0, 1):
                to = pl.ds(pl.multiple_of(h * 144 + i * 16, 16), 16)
                self.put(to, 0, self.r5[2 * h, at, :])
                self.put(to, self.cut, self.r5[2 * h + 1, at, :rest])

        for copy in self.c2 + self.c3 + self.c5 + self.c5b:
            copy.wait_send()
        if not self.direct:
            for copy in self.c3b:
                copy.wait_send()


def reduce_buffers(n, cut, computed):
    bufs = [
        pltpu.VMEM((2, 288, n), BF),
        pltpu.VMEM((288, n), BF),
        pltpu.VMEM((4, 144, cut), BF),
        pltpu.VMEM((3, 144, cut), BF),
        pltpu.VMEM((144, cut), BF),
        pltpu.VMEM((4, 144, cut), BF),
        pltpu.VMEM((144, cut), BF),
    ] + sems(20)
    return [pltpu.VMEM((2, 288, n), BF)] + bufs if computed else bufs


def norm_back(v, gain, dy):
    r = lax.rsqrt(jnp.mean(v * v, axis=-1, keepdims=True) + EPS)
    gdy = gain * dy
    dv = r * gdy - v * (r * r * r * jnp.mean(gdy * v, axis=-1, keepdims=True))
    return dv, r * v * dy


def turn_back(d, cosine, sine):
    d1, d2 = d[:, :128], d[:, 128:]
    return jnp.concatenate([d1 * cosine + d2 * sine, d2 * cosine - d1 * sine], axis=1)


class BackIn(NamedTuple):
    x: Any
    d_ffn_t: Any
    hidden: Any
    normed2_t: Any
    d_gate: Any
    d_up: Any
    middle: Any
    branch: Any
    cot: Any
    tokens: Any
    gains: Any
    dg3: Any
    attn: Any
    attn_low: Any
    lse: Any
    queries: Any
    kv: Any
    key_pos: Any
    query_pos: Any
    small: Any
    normed_t: Any
    q_proj: Any
    k_proj: Any
    heads: Any
    cosine: Any
    sine: Any

class BackOut(NamedTuple):
    grad_tokens: Any
    o_down: Any
    o_gate: Any
    o_up: Any
    o_q: Any
    o_o: Any
    o_k: Any
    o_v: Any
    o_last: Any


def back_kernel(*refs):
    n_in, n_out = len(BackIn._fields), len(BackOut._fields)
    i = BackIn(*refs[:n_in])
    o = BackOut(*refs[n_in : n_in + n_out])
    rest = list(refs[n_in + n_out :])

    def take(n):
        got = rest[:n]
        del rest[:n]
        return got

    p = Place()
    scale = HD ** (-0.5)
    total1 = take(1)[0]
    z1 = take(10)
    total2 = take(1)[0]
    z2 = take(5)
    (extra, xgot, d_mid, d_branch, d_attn, delta, dq, parts) = take(8)
    got_k, got_v, k_sum, v_sum, far_k, far_v = take(6)
    (kv_low, dn_kv, acc, gt, hg, oq, tail) = take(7)
    ks, kr, vs, vr, ks2, kr2, vs2, vr2, os, orr, xs, xr = take(12)
    down = Reduce(p, [o.o_down], take(10), 896, left=i.d_ffn_t, right=i.hidden)
    gate = Reduce(p, [o.o_gate], take(10), 896, left=i.normed2_t, right=i.d_gate)
    up = Reduce(p, [o.o_up], [down.sent] + take(9), 896, left=i.normed2_t, right=i.d_up)
    roq = Reduce(p, [o.o_q, o.o_o], take(9), 256, src=oq)
    rkv = Reduce(p, [o.o_k, o.o_v, o.o_last], take(9), 384, src=tail, direct=True)
    firsts = [ZSum(p, i.x, total1, 128 * h, *z1[5 * h : 5 * h + 5]) for h in (0, 1)]
    x2 = total1
    second = ZSum(p, x2, total2, 0, *z2)
    wq, wk, wv, wo = [slice(256 * j, 256 * j + 256) for j in range(4)]
    small = i.small

    greet(
        [p.sib(), p.dy(1), p.dy(3)]
        + [p.dc(d) for d in range(1, 8)]
        + [p.dz(d) for d in (1, 2, 3)]
    )
    for half in firsts:
        half.start()
    down.one()
    gate.one()
    acc[...] = jnp.zeros_like(acc)
    gt[...] = jnp.zeros_like(gt)
    hg[...] = jnp.zeros_like(hg)
    extra[...] = jnp.zeros_like(extra)
    firsts[0].middle()
    down.two()
    firsts[1].middle()
    gate.two()
    for copy in down.c1:
        copy.wait_send()
    up.one()
    for half in firsts:
        half.finish()

    @pl.loop(0, 16)
    def _(b):
        at = pl.ds(pl.multiple_of(b * 16, 16), 16)
        dm, dg = norm_back(
            i.middle[at, :], i.gains[2:3, :], total1[at, :].astype(F32)
        )
        acc[2] += dg
        dm = dm + i.cot[at, :].astype(F32)
        d_mid[at, :] = dm
        db, dg = norm_back(i.branch[at, :].astype(F32), i.gains[1:2, :], dm)
        acc[1] += dg
        d_branch[at, :] = db.astype(BF)

    down.three()
    d_attn[...] = plain(d_branch[...], small[:, wo]).astype(BF)
    delta[...] = jnp.sum(d_attn[...].astype(F32) * i.attn[...], axis=-1, keepdims=True)
    dq[...] = jnp.zeros_like(dq)
    up.two()

    def keys_block(kb):
        k, v = i.kv[kb, :, :HD], i.kv[kb, :, HD:]
        scores = against(i.queries[...], k) * scale
        seen = i.key_pos[kb] <= i.query_pos[...]
        probs = jnp.where(seen, jnp.exp(scores - i.lse[...]), 0.0)
        d_probs = against(d_attn[...], v)
        ds = (probs * (d_probs - delta[...])).astype(BF)
        dq[...] += plain(ds, k)
        dk = inner(ds, i.queries[...]) * scale
        dv = inner(probs.astype(BF), d_attn[...])
        parts[kb, :, :HD] = dk.astype(BF)
        parts[kb, :, HD:] = dv.astype(BF)

    def key_copy(kb, d, e):
        slot = 3 * (d % 8) + e - 1
        row = pl.ds(pl.multiple_of(((p.z + e) % 4) * 64, 64), 64)
        return pltpu.make_async_remote_copy(
            src_ref=parts.at[kb, row, pl.ds(0, HD)],
            dst_ref=got_k.at[e - 1, d % 8],
            send_sem=ks.at[slot],
            recv_sem=kr.at[slot],
            device_id=p.dz(e),
            device_id_type=MESH,
        )

    def value_copy(kb, d):
        return pltpu.make_async_remote_copy(
            src_ref=parts.at[kb, :, pl.ds(HD, HD)],
            dst_ref=got_v.at[d - 1],
            send_sem=vs.at[d - 1],
            recv_sem=vr.at[d - 1],
            device_id=(p.f, kb, p.z),
            device_id_type=MESH,
        )

    @pl.loop(1, 8)
    def _(d):
        kb = (p.c + d) % 8
        keys_block(kb)
        value_copy(kb, d).start()
        for e in (2, 1, 3):
            key_copy(kb, d, e).start()

    keys_block(p.c)
    for e in (2, 1, 3):
        key_copy(p.c, 0, e).start()

    gate.three()

    @pl.loop(0, 4)
    def _(b):
        at = pl.ds(pl.multiple_of(b * 64, 64), 64)
        dn = turn_back(dq[at, :] * scale, i.cosine[at, :], i.sine[at, :])
        dv, dg = norm_back(i.q_proj[at, :], i.heads[4:5, :], dn)
        acc[3, :, :HD] += dg.reshape(4, 16, HD).sum(axis=0)
        dq[at, :] = dv

    dq_low = dq[...].astype(BF)
    x2[...] = against(dq_low, small[:, wq]).astype(BF)
    extra[0:1, :] = jnp.sum(acc[3, :, :HD], axis=0, keepdims=True).astype(BF)
    second.start()
    more = [
        send(extra, xgot.at[d - 1], xs.at[d - 1], xr.at[d - 1], p.dz(d)) for d in (1, 2, 3)
    ]
    oq[:, :HD] = plain(i.normed_t[...], dq_low).astype(BF)
    oq[:, HD:] = inner(d_branch[...], i.attn_low[...]).astype(BF)
    roq.one()
    down.four()

    for d in range(8):
        for e in (1, 2, 3):
            key_copy(p.c, d, e).wait_recv()
    own = pl.ds(pl.multiple_of(p.z * 64, 64), 64)

    @pl.loop(0, 8)
    def _(d):
        kb = (p.c + d) % 8
        total = parts[kb, own, :HD].astype(F32)
        for e in range(3):
            total = total + got_k[e, d].astype(F32)
        k_sum[d] = total.astype(BF)

    keys_far = [
        send(k_sum.at[d], far_k.at[d - 1], ks2.at[d - 1], kr2.at[d - 1], p.dc(d))
        for d in range(1, 8)
    ]
    for d in range(1, 8):
        value_copy(p.c, d).wait_recv()

    @pl.loop(0, 16)
    def _(b):
        at = pl.ds(pl.multiple_of(b * 16, 16), 16)
        total = parts[p.c, at, HD:].astype(F32)
        for d in range(7):
            total = total + got_v[d, at, :].astype(F32)
        v_sum[at, :] = total.astype(BF)

    values_far = [
        send(
            v_sum.at[pl.ds(pl.multiple_of(((p.z + e) % 4) * 64, 64), 64)],
            far_v.at[e - 1],
            vs2.at[e - 1],
            vr2.at[e - 1],
            p.dz(e),
        )
        for e in (2, 1, 3)
    ]
    second.middle()
    down.fourb()
    up.three()
    gate.four()
    for copy in keys_far + values_far:
        copy.wait_recv()

    @pl.loop(0, 4)
    def _(b):
        at = pl.ds(pl.multiple_of(p.z * 64 + b * 16, 16), 16)
        to = pl.ds(pl.multiple_of(b * 16, 16), 16)
        total = k_sum[0, to, :].astype(F32)
        for d in range(7):
            total = total + far_k[d, to, :].astype(F32)
        kv_low[at, :HD] = total.astype(BF)
        total = v_sum[at, :].astype(F32)
        for e in range(3):
            total = total + far_v[e, to, :].astype(F32)
        kv_low[at, HD:] = total.astype(BF)

    kv2 = [
        send(kv_low.at[own], kv_low.at[own], os.at[d - 1], orr.at[d - 1], p.dz(d))
        for d in (2, 1, 3)
    ]
    down.five()
    roq.two()
    for copy in kv2:
        copy.wait_recv()
    acc[3] = jnp.zeros_like(acc[3])

    @pl.loop(0, 4)
    def _(b):
        at = pl.ds(pl.multiple_of(b * 64, 64), 64)
        dn = turn_back(kv_low[at, :HD].astype(F32), i.cosine[at, :], i.sine[at, :])
        dv, dg = norm_back(i.k_proj[at, :], i.heads[5:6, :], dn)
        acc[3, :, :HD] += dg.reshape(4, 16, HD).sum(axis=0)
        dq[at, :] = dv

    dk_low = dq[...].astype(BF)
    dn_kv[...] = against(dk_low, small[:, wk]) + against(kv_low[:, HD:], small[:, wv])
    tail[:, :HD] = plain(i.normed_t[...], dk_low).astype(BF)
    tail[:, HD : 2 * HD] = plain(i.normed_t[...], kv_low[:, HD:]).astype(BF)
    for copy in more:
        copy.wait()
    heads = extra[0:1, :].astype(F32)
    for d in range(3):
        heads = heads + xgot[d, 0:1, :].astype(F32)
    hg[4:5, :] = heads
    hg[5:6, :] = jnp.sum(acc[3, :, :HD], axis=0, keepdims=True)
    second.finish()

    @pl.loop(0, 16)
    def _(b):
        at = pl.ds(pl.multiple_of(b * 16, 16), 16)
        dn = total2[at, :].astype(F32) + dn_kv[at, :]
        dv, dg = norm_back(i.tokens[at, :].astype(F32), i.gains[0:1, :], dn)
        acc[0] += dg
        o.grad_tokens[at, :] = d_mid[at, :] + dv

    for g in range(3):
        gt[g : g + 1, :] = jnp.sum(acc[g], axis=0, keepdims=True)
    gt[3:4, :] = i.dg3[...]
    last = gt[...].T
    heads_t = hg[...].T
    tail[:, 2 * HD :] = last.astype(BF)
    for f in range(4):
        tail[288 * f : 288 * f + 64, 2 * HD :] = (
            last[288 * f : 288 * f + 64] + heads_t[64 * f : 64 * f + 64]
        ).astype(BF)
    rkv.one()
    up.four()
    gate.fourb()
    rkv.two()
    roq.three()
    down.fiveb()
    up.fourb()
    rkv.three()
    roq.four()
    gate.five()
    rkv.four()
    rkv.fourb()
    roq.fourb()
    up.five()
    gate.fiveb()
    down.six()
    rkv.five()
    rkv.fiveb()
    roq.five()
    up.fiveb()
    gate.six()
    roq.fiveb()
    rkv.six()
    roq.six()
    up.six()
    for d in range(8):
        for e in (1, 2, 3):
            key_copy(p.c, d, e).wait_send()
    for d in range(1, 8):
        value_copy(p.c, d).wait_send()
    for copy in kv2 + keys_far + values_far + gate.c1 + up.c1 + roq.c1 + rkv.c1:
        copy.wait_send()


def zsum_buffers(share):
    return [pltpu.VMEM((3, share, 1152), BF)] + sems(3) + sems(3)


def back_call(ins, cid):
    scratch = (
        [pltpu.VMEM((256, 1152), BF)]
        + zsum_buffers(32) * 2
        + [pltpu.VMEM((256, 1152), BF)]
        + zsum_buffers(64)
        + [
            pltpu.VMEM((16, HD), BF),
            pltpu.VMEM((3, 16, HD), BF),
            pltpu.VMEM((256, 1152), F32),
            pltpu.VMEM((256, 1152), BF),
            pltpu.VMEM((256, HD), BF),
            pltpu.VMEM((256, 1), F32),
            pltpu.VMEM((256, HD), F32),
            pltpu.VMEM((8, 256, 2 * HD), BF),
            pltpu.VMEM((3, 8, 64, HD), BF),
            pltpu.VMEM((7, 256, HD), BF),
            pltpu.VMEM((8, 64, HD), BF),
            pltpu.VMEM((256, HD), BF),
            pltpu.VMEM((7, 64, HD), BF),
            pltpu.VMEM((3, 64, HD), BF),
            pltpu.VMEM((256, 2 * HD), BF),
            pltpu.VMEM((256, 1152), F32),
            pltpu.VMEM((4, 16, 1152), F32),
            pltpu.VMEM((128, 1152), F32),
            pltpu.VMEM((128, HD), F32),
            pltpu.VMEM((1152, 512), BF),
            pltpu.VMEM((1152, 640), BF),
        ]
        + sems(24)
        + sems(7)
        + sems(7)
        + sems(3)
        + sems(3)
        + sems(3)
        + reduce_buffers(1728, 896, True) * 2
        + reduce_buffers(1728, 896, False)
        + reduce_buffers(512, 256, False)
        + reduce_buffers(640, 384, False)
    )
    shapes = [((256, 1152), F32)] + [((288, n), BF) for n in (1728, 1728, 1728, 256, 256, 256, 256, 128)]
    return pl.pallas_call(
        back_kernel,
        out_shape=[jax.ShapeDtypeStruct(*shape) for shape in shapes],
        in_specs=[VM] * len(ins),
        out_specs=[VM] * len(shapes),
        scratch_shapes=scratch,
        compiler_params=params(cid, 62),
        name="backward",
    )(*ins)


class ForeIn(NamedTuple):
    tokens: Any
    cot: Any
    w_query: Any
    w_key: Any
    w_value: Any
    w_out: Any
    columns: Any
    w_gate: Any
    w_up: Any
    w_down: Any
    cosine: Any
    sine: Any
    key_pos: Any
    query_pos: Any

class ForeOut(NamedTuple):
    out: Any
    small: Any
    gains: Any
    heads: Any
    x: Any
    d_ffn_t: Any
    hidden: Any
    normed2_t: Any
    d_gate: Any
    d_up: Any
    middle: Any
    branch: Any
    dg3: Any
    attn: Any
    attn_low: Any
    lse: Any
    queries: Any
    kv: Any
    normed_t: Any
    q_proj: Any
    k_proj: Any

TILES = [(c0, min(c0 + 256, 1728)) for c0 in range(0, 1728, 256)]


def turn(v, cosine, sine):
    v1, v2 = v[:, :128], v[:, 128:]
    return jnp.concatenate([v1 * cosine - v2 * sine, v2 * cosine + v1 * sine], axis=1)


def transpose_into(dst, src):
    for c0 in range(0, 1152, 128):
        dst[c0 : c0 + 128, :] = src[:, c0 : c0 + 128].astype(F32).T.astype(BF)


def fore_kernel(*refs):
    n_in, n_out = len(ForeIn._fields), len(ForeOut._fields)
    i = ForeIn(*refs[:n_in])
    o = ForeOut(*refs[n_in : n_in + n_out])
    rest = list(refs[n_in + n_out :])

    def take(n):
        got = rest[:n]
        del rest[:n]
        return got

    p = Place()
    scale = HD ** (-0.5)
    w_gate, w_up, w_down, act, slope, normed, d_ffn, probs, head_cols, accg = take(10)
    local, gs, gr, ks, kr, vs, vr, fs, fr = take(9)
    total1, total2 = take(2)
    z1, z2 = take(10), take(10)
    part, pack = take(2)
    small = o.small
    halves = [(h, slice(128 * h, 128 * h + 128)) for h in (0, 1)]
    firsts = [ZSum(p, part, total1, 128 * h, *z1[5 * h : 5 * h + 5]) for h in (0, 1)]
    seconds = [ZSum(p, part, total2, 128 * h, *z2[5 * h : 5 * h + 5]) for h in (0, 1)]
    kv = o.kv
    gathers = [
        Gather(p, src, dst, local.at[j], gs, gr, 6 * j, j > 0)
        for j, (src, dst) in enumerate(
            [(pack, small), (i.w_gate, w_gate), (i.w_up, w_up), (i.w_down, w_down)]
        )
    ]
    g_small, g_gate, g_up, g_down = gathers

    greet([p.sib(), p.dy(1), p.dy(3)] + [p.dc(d) for d in range(1, 8)] + [p.dz(d) for d in (1, 2, 3)])
    for ref, c0 in ((i.w_query, 0), (i.w_key, 256), (i.w_value, 512), (i.w_out, 768)):
        pack[:, c0 : c0 + 256] = ref[...]
    pack[:, 1024:] = i.columns[...]
    g_small.start()
    g_small.start_far()
    g_gate.start()
    g_up.start()
    g_down.start()
    accg[...] = jnp.zeros_like(accg)
    g_small.forward()
    g_gate.start_far()
    g_small.finish()

    o.gains[...] = small[:, 1024:].astype(F32).T[:8, :]
    for f in range(4):
        head_cols[64 * f : 64 * f + 64, :] = small[288 * f : 288 * f + 64, 1024:].astype(F32)
    o.heads[...] = head_cols[...].T[:8, :]

    @pl.loop(0, 16)
    def _(b):
        at = pl.ds(pl.multiple_of(b * 16, 16), 16)
        normed[at, :] = normalize(i.tokens[at, :].astype(F32), o.gains[0:1, :]).astype(BF)

    o.q_proj[...] = plain(normed[...], small[:, :256])
    o.k_proj[...] = plain(normed[...], small[:, 256:512])
    kv[p.c, :, HD:] = plain(normed[...], small[:, 512:768]).astype(BF)

    quarter = pl.ds(pl.multiple_of(p.z * 64, 64), 64)
    sent = [
        send(
            kv.at[p.c, quarter, pl.ds(HD, HD)],
            kv.at[p.c, quarter, pl.ds(HD, HD)],
            vs.at[d - 1],
            vr.at[d - 1],
            p.dc(d),
        )
        for d in range(1, 8)
    ]

    @pl.loop(0, 4)
    def _(b):
        at = pl.ds(pl.multiple_of(b * 64, 64), 64)
        n = normalize(o.k_proj[at, :], o.heads[5:6, :])
        kv[p.c, at, :HD] = turn(n, i.cosine[at, :], i.sine[at, :]).astype(BF)

    keys = kv.at[p.c, :, pl.ds(0, HD)]
    sent_k = [send(keys, keys, ks.at[d - 1], kr.at[d - 1], p.dc(d)) for d in range(1, 8)]

    @pl.loop(0, 4)
    def _(b):
        at = pl.ds(pl.multiple_of(b * 64, 64), 64)
        n = normalize(o.q_proj[at, :], o.heads[4:5, :])
        o.queries[at, :] = turn(n, i.cosine[at, :], i.sine[at, :]).astype(BF)

    g_gate.across()
    g_up.start_far()
    for copy in sent:
        copy.wait_recv()
    sent_z = []
    for d in range(8):
        block = kv.at[(p.c + 8 - d) % 8, quarter, pl.ds(HD, HD)]
        if d == 0:
            continue
        sent_z += [
            send(block, block, fs.at[3 * d + e - 1], fr.at[3 * d + e - 1], p.dz(e))
            for e in (2, 1, 3)
        ]
    transpose_into(o.normed_t, normed)
    for copy in sent_k:
        copy.wait_recv()
    g_gate.forward()
    g_down.start_far()

    @pl.loop(0, 4)
    def _(b):
        at = pl.ds(pl.multiple_of(b * 64, 64), 64)
        query = o.queries[at, :]
        seen = [i.key_pos[kb] <= i.query_pos[at, :] for kb in range(8)]
        scores = [against(query, kv[kb, :, :HD]) * scale for kb in range(8)]
        top = jnp.max(jnp.where(seen[0], scores[0], -1e30), axis=-1, keepdims=True)
        for kb in range(1, 8):
            top = jnp.maximum(
                top, jnp.max(jnp.where(seen[kb], scores[kb], -1e30), axis=-1, keepdims=True)
            )
        scores = [jnp.where(seen[kb], jnp.exp(scores[kb] - top), 0.0) for kb in range(8)]
        total = jnp.sum(scores[0], axis=-1, keepdims=True)
        for kb in range(1, 8):
            total = total + jnp.sum(scores[kb], axis=-1, keepdims=True)
        o.lse[at, :] = top + jnp.log(total)
        share = 1.0 / total
        for kb in range(8):
            probs[kb, at, :] = (scores[kb] * share).astype(BF)

    g_up.across()
    for copy in sent_z:
        copy.wait_recv()
    attn = plain(probs[0], kv[0, :, HD:])
    for kb in range(1, 8):
        attn = attn + plain(probs[kb], kv[kb, :, HD:])
    o.attn[...] = attn
    attn_low = attn.astype(BF)
    o.attn_low[...] = attn_low
    for h, rows in halves:
        part[rows, :] = against(attn_low[rows], small[:, 768:1024]).astype(BF)
        firsts[h].start()
    g_up.forward()
    g_down.across()
    for half in firsts:
        half.middle()
    g_gate.finish()

    def middle_rows(b):
        at = pl.ds(pl.multiple_of(b * 16, 16), 16)
        branch = total1[at, :]
        o.branch[at, :] = branch
        middle = i.tokens[at, :].astype(F32) + normalize(
            branch.astype(F32), o.gains[1:2, :]
        )
        o.middle[at, :] = middle
        normed[at, :] = normalize(middle, o.gains[2:3, :]).astype(BF)

    for h, rows in halves:
        firsts[h].finish()
        pl.loop(8 * h, 8 * h + 8)(middle_rows)
    g_up.finish()
    for c0, c1 in TILES:
        gate = plain(normed[...], w_gate[:, c0:c1])
        up = plain(normed[...], w_up[:, c0:c1])
        bend = jnp.tanh(0.7978845608028654 * (gate + 0.044715 * gate * gate * gate))
        gelu = 0.5 * gate * (1.0 + bend)
        o.hidden[:, c0:c1] = (gelu * up).astype(BF)
        act[:, c0:c1] = gelu
        rise = 0.7978845608028654 * (1.0 + 0.134145 * gate * gate)
        slope[:, c0:c1] = up * (0.5 * (1.0 + bend) + 0.5 * gate * (1.0 - bend * bend) * rise)
    g_down.forward()
    g_down.finish()
    for h, rows in halves:
        for c0 in range(0, 1152, 384):
            part[rows, c0 : c0 + 384] = against(
                o.hidden[rows, :], w_down[c0 : c0 + 384, :]
            ).astype(BF)
        seconds[h].start()
    transpose_into(o.normed2_t, normed)
    for half in seconds:
        half.middle()

    def last_rows(b):
        at = pl.ds(pl.multiple_of(b * 16, 16), 16)
        ffn = total2[at, :].astype(F32)
        o.out[at, :] = (o.middle[at, :] + normalize(ffn, o.gains[3:4, :])).astype(BF)
        dv, dg = norm_back(ffn, o.gains[3:4, :], i.cot[at, :].astype(F32))
        accg[...] += dg
        d_ffn[at, :] = dv.astype(BF)

    for h, rows in halves:
        seconds[h].finish()
        pl.loop(8 * h, 8 * h + 8)(last_rows)
    o.dg3[...] = jnp.sum(accg[...], axis=0, keepdims=True)
    transpose_into(o.d_ffn_t, d_ffn)
    for c0, c1 in TILES:
        d_hidden = plain(d_ffn[...], w_down[:, c0:c1])
        o.d_up[:, c0:c1] = (d_hidden * act[:, c0:c1]).astype(BF)
        o.d_gate[:, c0:c1] = (d_hidden * slope[:, c0:c1]).astype(BF)
    for c0 in range(0, 1152, 384):
        o.x[:, c0 : c0 + 384] = (
            against(o.d_gate[...], w_gate[c0 : c0 + 384, :])
            + against(o.d_up[...], w_up[c0 : c0 + 384, :])
        ).astype(BF)
    for copy in sent + sent_k + sent_z:
        copy.wait_send()


def fore_call(ins, cid):
    scratch = (
        [pltpu.VMEM((1152, 1728), BF)] * 3
        + [
            pltpu.VMEM((256, 1728), F32),
            pltpu.VMEM((256, 1728), F32),
            pltpu.VMEM((256, 1152), BF),
            pltpu.VMEM((256, 1152), BF),
            pltpu.VMEM((8, 256, 256), BF),
            pltpu.VMEM((256, 128), F32),
            pltpu.VMEM((16, 1152), F32),
            pltpu.SemaphoreType.DMA((4,)),
        ]
        + sems(24)
        + sems(7)
        + sems(7)
        + sems(24)
        + [pltpu.VMEM((256, 1152), BF)] * 2
        + zsum_buffers(32) * 4
        + [pltpu.VMEM((256, 1152), BF), pltpu.VMEM((288, 1152), BF)]
    )
    shapes = ForeOut(
        out=((256, 1152), BF),
        small=((1152, 1152), BF),
        gains=((8, 1152), F32),
        heads=((8, 256), F32),
        x=((256, 1152), BF),
        d_ffn_t=((1152, 256), BF),
        hidden=((256, 1728), BF),
        normed2_t=((1152, 256), BF),
        d_gate=((256, 1728), BF),
        d_up=((256, 1728), BF),
        middle=((256, 1152), F32),
        branch=((256, 1152), BF),
        dg3=((1, 1152), F32),
        attn=((256, 256), F32),
        attn_low=((256, 256), BF),
        lse=((256, 1), F32),
        queries=((256, 256), BF),
        kv=((8, 256, 512), BF),
        normed_t=((1152, 256), BF),
        q_proj=((256, 256), F32),
        k_proj=((256, 256), F32),
    )
    done = pl.pallas_call(
        fore_kernel,
        out_shape=[jax.ShapeDtypeStruct(*shape) for shape in shapes],
        in_specs=[VM] * len(ins),
        out_specs=[VM] * len(shapes),
        scratch_shapes=scratch,
        compiler_params=params(cid, 62),
        name="forward",
    )(*ins)
    return ForeOut(*done)


def final_kernel(*refs):
    ins, outs = refs[:10], refs[10:21]
    held, wide, (rows_ref, heads_ref, s_in, s_out) = refs[21:31], refs[31:38], refs[38:]
    loads = [pltpu.make_async_copy(ins[n], held[n], s_in.at[n]) for n in range(10)]
    for copy in loads:
        copy.start()
    stores = []
    for n in range(9):
        loads[n].wait()
        if n > 1:
            wide[n - 2][...] = held[n][...].astype(F32)
        copy = pltpu.make_async_copy(held[n] if n < 2 else wide[n - 2], outs[n], s_out.at[n])
        copy.start()
        stores.append(copy)
    loads[9].wait()
    columns = held[9][...].astype(F32).T
    rows_ref[...] = columns[:4, :]
    heads_ref[...] = columns[4:6, :64]
    for n, ref in ((9, rows_ref), (10, heads_ref)):
        copy = pltpu.make_async_copy(ref, outs[n], s_out.at[n])
        copy.start()
        stores.append(copy)
    for copy in stores:
        copy.wait()


def final_call(*ins):
    grads = [a.shape for a in ins[2:9]]
    shapes = [ins[0].shape, ins[1].shape] + grads + [(4, 288), (2, 64)]
    any_space = pl.BlockSpec(memory_space=pl.ANY)
    return pl.pallas_call(
        final_kernel,
        out_shape=[
            jax.ShapeDtypeStruct(shape, BF if n == 0 else F32) for n, shape in enumerate(shapes)
        ],
        in_specs=[any_space] * 10,
        out_specs=[any_space] * 11,
        scratch_shapes=[pltpu.VMEM(a.shape, a.dtype) for a in ins]
        + [pltpu.VMEM(shape, F32) for shape in grads]
        + [
            pltpu.VMEM((4, 288), F32),
            pltpu.VMEM((2, 64), F32),
            pltpu.SemaphoreType.DMA((10,)),
            pltpu.SemaphoreType.DMA((11,)),
        ],
        compiler_params=pltpu.CompilerParams(vmem_limit_bytes=62 * 2**20),
        name="final",
    )(*ins)


def per_device(
    tokens,
    block_order,
    cotangent,
    w_query,
    w_key,
    w_value,
    w_out,
    w_gate,
    w_up,
    w_down,
    gains,
    head_gains,
):
    _, rows, width = tokens.shape
    cycle_index = lax.axis_index("context")
    span = rows // 2
    seq_len = rows * 8

    columns = jnp.pad(
        jnp.concatenate([gains.T, jnp.pad(head_gains.T, ((0, 288 - 64), (0, 0)))], axis=1),
        ((0, 0), (0, 122)),
    )
    offsets = jnp.arange(seq_len, dtype=jnp.int32)
    key_pos = (jnp.repeat(block_order, span, axis=1) * span + (offsets % span)[None, :])[0]
    query_pos = lax.dynamic_slice_in_dim(key_pos, cycle_index * rows, rows, 0)
    cosine, sine = tables(query_pos)
    ins = ForeIn(
        tokens=tokens[0],
        cot=cotangent[0],
        w_query=w_query,
        w_key=w_key,
        w_value=w_value,
        w_out=w_out.T,
        columns=columns,
        w_gate=w_gate,
        w_up=w_up,
        w_down=w_down.T,
        cosine=cosine,
        sine=sine,
        key_pos=key_pos.reshape(8, 1, rows),
        query_pos=query_pos[:, None],
    )
    held = fore_call(ins, 1)
    grad_tokens, sum_down, sum_gate, sum_up, sum_q, sum_o, sum_k, sum_v, last = back_call(
        BackIn(
            x=held.x,
            d_ffn_t=held.d_ffn_t,
            hidden=held.hidden,
            normed2_t=held.normed2_t,
            d_gate=held.d_gate,
            d_up=held.d_up,
            middle=held.middle,
            branch=held.branch,
            cot=ins.cot,
            tokens=ins.tokens,
            gains=held.gains,
            dg3=held.dg3,
            attn=held.attn,
            attn_low=held.attn_low,
            lse=held.lse,
            queries=held.queries,
            kv=held.kv,
            key_pos=ins.key_pos,
            query_pos=ins.query_pos,
            small=held.small,
            normed_t=held.normed_t,
            q_proj=held.q_proj,
            k_proj=held.k_proj,
            heads=held.heads,
            cosine=ins.cosine,
            sine=ins.sine,
        ),
        2,
    )
    done = final_call(
        held.out, grad_tokens, sum_gate, sum_up, sum_down, sum_q, sum_k, sum_v, sum_o, last
    )
    result, d_tokens, d_gate, d_up, d_down, d_q, d_k, d_v, d_o, d_gains, d_heads = done
    return (
        result[None],
        d_tokens[None],
        d_q,
        d_k,
        d_v,
        d_o.T,
        d_gate,
        d_up,
        d_down.T,
        d_gains,
        d_heads,
    )


def solution(mesh):
    in_specs = (
        P("fsdp", "context", None),
        P("fsdp", None),
        P("fsdp", "context", None),
        P("fsdp", "tensor"),
        P("fsdp", None),
        P("fsdp", None),
        P("tensor", "fsdp"),
        P("fsdp", "tensor"),
        P("fsdp", "tensor"),
        P("tensor", "fsdp"),
        P(None, "fsdp"),
        P(None, "fsdp"),
    )
    out_specs = (
        P("fsdp", "context", None),
        P("fsdp", "context", None),
        P("fsdp", "tensor"),
        P("fsdp", None),
        P("fsdp", None),
        P("tensor", "fsdp"),
        P("fsdp", "tensor"),
        P("fsdp", "tensor"),
        P("tensor", "fsdp"),
        P(None, "fsdp"),
        P(None, "fsdp"),
    )
    return jax.shard_map(
        per_device, mesh=mesh, in_specs=in_specs, out_specs=out_specs, check_vma=False
    )
```

time: 290 us -> 240 us (0.83)
  Pallas kernels: 263 us -> 234 us
  local copies, waits for them, and re-layouts: 20.1 us -> 1.82 us
    pallas_call x2 -> x3, Pallas kernels: 263 us -> 234 us  [the longest x1 129 us: back_call(): pl.pallas_call(back_kernel, out_shape=[jax.ShapeDtypeStruct(*shape) for s...]
    unnamed x21 -> x0, local copies, waits for them, and re-layouts: 14.8 us -> none
    transpose x3 -> x0, local copies, waits for them, and re-layouts: 4.11 us -> none  [the longest x1 2.26 us: per_device(): sum_oq[:, HD:]]
where the time goes in v2:
time: 240 us
  Pallas kernels  234 us (98%)
  other arithmetic  3.26 us (1%)
    pallas_call x1, Pallas kernels, back_call(): pl.pallas_call(back_kernel, out_shape=[jax.ShapeDtypeStruct(*shape) for s...  129 us
    pallas_call x1, Pallas kernels, fore_call(): pl.pallas_call(fore_kernel, out_shape=[jax.ShapeDtypeStruct(*shape) for s...  99.3 us
    pallas_call x1, Pallas kernels, final_call(): pl.pallas_call(final_kernel, out_shape=[jax.ShapeDtypeStruct(shape, BF if...  5.05 us

profile of v2, /device:TPU:0, one launch (start us, length us, event | category | flops | bytes accessed | tf_op | source)
XLA Modules:
  0.0 239.6 jit_solution(8221810988911555938)
XLA Ops:
  0.7 0.7 multiply_reduce_fusion
  1.3 0.1 mul.78
  1.4 0.1 broadcast_in_dim.16
  1.5 0.6 fusion.1.refs_12_.refs_17_
  2.1 0.7 fusion.3
  2.8 0.1 broadcast_in_dim.15
  2.9 0.1 copy.29
  3.0 0.7 pad.9.refs_6_
  3.7 0.8 copy.30.refs_13_.refs_18_
  4.5 1.2 multiply_sine_fusion
  5.7 99.3 %forward.1 = (bf16[256,1152]{1,0:T(8,128)(2,1)}, bf16[1152,1152]{1,0:T(8,128)(2,1)}, f32[8,1152]{1,0:T(8,128)}, f32[8,256]{1,0:T(8,128)}, bf16[256,1152]{1,0:T(8...) custom-call(bf16[256,1152]{1,0:T(8,128)(2,1)} %bitcast.16, ...), custom_call_target="tpu_custom_call" | custom-call | tf_op jit(solution)/shard_map/forward/pallas_call | solution.py:1118
  105.0 129.3 %backward.1 = (f32[256,1152]{1,0:T(8,128)}, bf16[288,1728]{1,0:T(8,128)(2,1)}, bf16[288,1728]{1,0:T(8,128)(2,1)}, bf16[288,1728]{1,0:T(8,128)(2,1)}, bf16[288,25...) custom-call(bf16[256,1152]{1,0:T(8,128)(2,1)} %get-tuple-element.53., ...), custom_call_target="tpu_custom_call" | custom-call | tf_op jit(solution)/shard_map/backward/pallas_call | solution.py:807
  234.3 5.0 %final.1 = (bf16[256,1152]{1,0:T(8,128)(2,1)}, f32[256,1152]{1,0:T(8,128)}, f32[288,1728]{1,0:T(8,128)}, f32[288,1728]{1,0:T(8,128)}, f32[288,1728]{1,0:T(8,128)...) custom-call(bf16[256,1152]{1,0:T(8,128)(2,1)} %get-tuple-element.52., ...), custom_call_target="tpu_custom_call" | custom-call | tf_op jit(solution)/shard_map/final/pallas_call | solution.py:1160
  (2 shorter events, 0.0 us)

commit v3 on v2

--- a/solution.py
+++ b/solution.py
@@ -105,6 +105,7 @@
 
 
 VM = pl.BlockSpec(memory_space=pltpu.VMEM)
+HB = pl.BlockSpec(memory_space=pl.ANY)
 
 
 def params(cid, limit=48):
@@ -454,7 +455,6 @@
     queries: Any
     kv: Any
     key_pos: Any
-    query_pos: Any
     small: Any
     normed_t: Any
     q_proj: Any
@@ -477,7 +477,6 @@
 
 def back_kernel(*refs):
     n_in, n_out = len(BackIn._fields), len(BackOut._fields)
-    i = BackIn(*refs[:n_in])
     o = BackOut(*refs[n_in : n_in + n_out])
     rest = list(refs[n_in + n_out :])
 
@@ -486,9 +485,17 @@
         del rest[:n]
         return got
 
+    i = BackIn(*take(n_in))
+    loading = take(1)[0]
+    loads = BackIn(
+        *[pltpu.make_async_copy(refs[n], i[n], loading.at[n]) for n in range(n_in)]
+    )
+    for copy in loads:
+        copy.start()
     p = Place()
     scale = HD ** (-0.5)
     total1 = take(1)[0]
+    own_pos = take(1)[0]
     z1 = take(10)
     total2 = take(1)[0]
     z2 = take(5)
@@ -504,7 +511,7 @@
     firsts = [ZSum(p, i.x, total1, 128 * h, *z1[5 * h : 5 * h + 5]) for h in (0, 1)]
     x2 = total1
     second = ZSum(p, x2, total2, 0, *z2)
-    wq, wk, wv, wo = [slice(256 * j, 256 * j + 256) for j in range(4)]
+    wq, wk, wv, wo = [slice(c0, c0 + 256) for c0 in (0, 256, 512, 896)]
     small = i.small
 
     greet(
@@ -512,8 +519,11 @@
         + [p.dc(d) for d in range(1, 8)]
         + [p.dz(d) for d in (1, 2, 3)]
     )
+    loads.x.wait()
     for half in firsts:
         half.start()
+    for copy in loads[1:]:
+        copy.wait()
     down.one()
     gate.one()
     acc[...] = jnp.zeros_like(acc)
@@ -530,7 +540,7 @@
     for half in firsts:
         half.finish()
 
-    @pl.loop(0, 16)
+    @pl.loop(0, 16, unroll=4)
     def _(b):
         at = pl.ds(pl.multiple_of(b * 16, 16), 16)
         dm, dg = norm_back(
@@ -543,6 +553,7 @@
         acc[1] += dg
         d_branch[at, :] = db.astype(BF)
 
+    own_pos[...] = jnp.broadcast_to(i.key_pos[p.c], (8, 256)).T[:, 0:1]
     down.three()
     d_attn[...] = plain(d_branch[...], small[:, wo]).astype(BF)
     delta[...] = jnp.sum(d_attn[...].astype(F32) * i.attn[...], axis=-1, keepdims=True)
@@ -552,7 +563,7 @@
     def keys_block(kb):
         k, v = i.kv[kb, :, :HD], i.kv[kb, :, HD:]
         scores = against(i.queries[...], k) * scale
-        seen = i.key_pos[kb] <= i.query_pos[...]
+        seen = i.key_pos[kb] <= own_pos[...]
         probs = jnp.where(seen, jnp.exp(scores - i.lse[...]), 0.0)
         d_probs = against(d_attn[...], v)
         ds = (probs * (d_probs - delta[...])).astype(BF)
@@ -596,6 +607,7 @@
     for e in (2, 1, 3):
         key_copy(p.c, 0, e).start()
 
+    down.four()
     gate.three()
 
     @pl.loop(0, 4)
@@ -613,10 +625,12 @@
     more = [
         send(extra, xgot.at[d - 1], xs.at[d - 1], xr.at[d - 1], p.dz(d)) for d in (1, 2, 3)
     ]
+    up.three()
     oq[:, :HD] = plain(i.normed_t[...], dq_low).astype(BF)
     oq[:, HD:] = inner(d_branch[...], i.attn_low[...]).astype(BF)
     roq.one()
-    down.four()
+    down.fourb()
+    gate.four()
 
     for d in range(8):
         for e in (1, 2, 3):
@@ -638,7 +652,7 @@
     for d in range(1, 8):
         value_copy(p.c, d).wait_recv()
 
-    @pl.loop(0, 16)
+    @pl.loop(0, 16, unroll=4)
     def _(b):
         at = pl.ds(pl.multiple_of(b * 16, 16), 16)
         total = parts[p.c, at, HD:].astype(F32)
@@ -657,9 +671,9 @@
         for e in (2, 1, 3)
     ]
     second.middle()
-    down.fourb()
-    up.three()
-    gate.four()
+    down.five()
+    gate.fourb()
+    roq.two()
     for copy in keys_far + values_far:
         copy.wait_recv()
 
@@ -680,8 +694,8 @@
         send(kv_low.at[own], kv_low.at[own], os.at[d - 1], orr.at[d - 1], p.dz(d))
         for d in (2, 1, 3)
     ]
-    down.five()
-    roq.two()
+    up.four()
+    down.fiveb()
     for copy in kv2:
         copy.wait_recv()
     acc[3] = jnp.zeros_like(acc[3])
@@ -698,6 +712,9 @@
     dn_kv[...] = against(dk_low, small[:, wk]) + against(kv_low[:, HD:], small[:, wv])
     tail[:, :HD] = plain(i.normed_t[...], dk_low).astype(BF)
     tail[:, HD : 2 * HD] = plain(i.normed_t[...], kv_low[:, HD:]).astype(BF)
+    gate.five()
+    up.fourb()
+    roq.three()
     for copy in more:
         copy.wait()
     heads = extra[0:1, :].astype(F32)
@@ -707,7 +724,7 @@
     hg[5:6, :] = jnp.sum(acc[3, :, :HD], axis=0, keepdims=True)
     second.finish()
 
-    @pl.loop(0, 16)
+    @pl.loop(0, 16, unroll=4)
     def _(b):
         at = pl.ds(pl.multiple_of(b * 16, 16), 16)
         dn = total2[at, :].astype(F32) + dn_kv[at, :]
@@ -726,30 +743,24 @@
             last[288 * f : 288 * f + 64] + heads_t[64 * f : 64 * f + 64]
         ).astype(BF)
     rkv.one()
-    up.four()
-    gate.fourb()
+    roq.four()
+    gate.fiveb()
+    up.five()
     rkv.two()
-    roq.three()
-    down.fiveb()
-    up.fourb()
+    roq.fourb()
+    down.six()
     rkv.three()
-    roq.four()
-    gate.five()
+    up.fiveb()
+    roq.five()
     rkv.four()
     rkv.fourb()
-    roq.fourb()
-    up.five()
-    gate.fiveb()
-    down.six()
+    roq.fiveb()
+    gate.six()
     rkv.five()
     rkv.fiveb()
-    roq.five()
-    up.fiveb()
-    gate.six()
-    roq.fiveb()
+    up.six()
+    roq.six()
     rkv.six()
-    roq.six()
-    up.six()
     for d in range(8):
         for e in (1, 2, 3):
             key_copy(p.c, d, e).wait_send()
@@ -765,7 +776,9 @@
 
 def back_call(ins, cid):
     scratch = (
-        [pltpu.VMEM((256, 1152), BF)]
+        [pltpu.VMEM(a.shape, a.dtype) for a in ins]
+        + [pltpu.SemaphoreType.DMA((len(ins),))]
+        + [pltpu.VMEM((256, 1152), BF), pltpu.VMEM((256, 1), F32)]
         + zsum_buffers(32) * 2
         + [pltpu.VMEM((256, 1152), BF)]
         + zsum_buffers(64)
@@ -807,7 +820,7 @@
     return pl.pallas_call(
         back_kernel,
         out_shape=[jax.ShapeDtypeStruct(*shape) for shape in shapes],
-        in_specs=[VM] * len(ins),
+        in_specs=[HB] * len(ins),
         out_specs=[VM] * len(shapes),
         scratch_shapes=scratch,
         compiler_params=params(cid, 62),
@@ -822,14 +835,14 @@
     w_key: Any
     w_value: Any
     w_out: Any
-    columns: Any
+    scales: Any
+    head_scales: Any
     w_gate: Any
     w_up: Any
     w_down: Any
     cosine: Any
     sine: Any
     key_pos: Any
-    query_pos: Any
 
 class ForeOut(NamedTuple):
     out: Any
@@ -870,7 +883,6 @@
 def fore_kernel(*refs):
     n_in, n_out = len(ForeIn._fields), len(ForeOut._fields)
     i = ForeIn(*refs[:n_in])
-    o = ForeOut(*refs[n_in : n_in + n_out])
     rest = list(refs[n_in + n_out :])
 
     def take(n):
@@ -878,32 +890,52 @@
         del rest[:n]
         return got
 
+    o = ForeOut(*take(n_out))
+    leaving = take(1)[0]
+    leave = ForeOut(
+        *[
+            pltpu.make_async_copy(o[n], refs[n_in + n], leaving.at[n])
+            for n in range(n_out)
+        ]
+    )
     p = Place()
     scale = HD ** (-0.5)
     w_gate, w_up, w_down, act, slope, normed, d_ffn, probs, head_cols, accg = take(10)
     local, gs, gr, ks, kr, vs, vr, fs, fr = take(9)
     total1, total2 = take(2)
     z1, z2 = take(10), take(10)
-    part, pack = take(2)
+    part, pack, rows_up, own_pos = take(4)
     small = o.small
     halves = [(h, slice(128 * h, 128 * h + 128)) for h in (0, 1)]
     firsts = [ZSum(p, part, total1, 128 * h, *z1[5 * h : 5 * h + 5]) for h in (0, 1)]
     seconds = [ZSum(p, part, total2, 128 * h, *z2[5 * h : 5 * h + 5]) for h in (0, 1)]
     kv = o.kv
     gathers = [
-        Gather(p, src, dst, local.at[j], gs, gr, 6 * j, j > 0)
+        Gather(p, src, dst, local.at[j], gs, gr, 6 * j, 0 < j < 4)
         for j, (src, dst) in enumerate(
-            [(pack, small), (i.w_gate, w_gate), (i.w_up, w_up), (i.w_down, w_down)]
+            [
+                (pack.at[:, pl.ds(0, 896)], small.at[:, pl.ds(0, 896)]),
+                (i.w_gate, w_gate),
+                (i.w_up, w_up),
+                (i.w_down, w_down),
+                (pack.at[:, pl.ds(896, 256)], small.at[:, pl.ds(896, 256)]),
+            ]
         )
     ]
-    g_small, g_gate, g_up, g_down = gathers
-
+    g_small, g_gate, g_up, g_down, g_out = gathers
+
+    for ref, c0 in ((i.w_query, 0), (i.w_key, 256), (i.w_value, 512), (i.w_out, 896)):
+        pack[:, c0 : c0 + 256] = ref[...]
+    rows_up[...] = jnp.zeros_like(rows_up)
+    rows_up[0:4, 0:288] = i.scales[...].astype(F32)
+    rows_up[4:6, 0:64] = i.head_scales[...].astype(F32)
+    pack[:, 768:896] = rows_up[...].T[:288, :].astype(BF)
+    own_pos[...] = jnp.broadcast_to(i.key_pos[p.c], (8, 256)).T[:, 0:1]
     greet([p.sib(), p.dy(1), p.dy(3)] + [p.dc(d) for d in range(1, 8)] + [p.dz(d) for d in (1, 2, 3)])
-    for ref, c0 in ((i.w_query, 0), (i.w_key, 256), (i.w_value, 512), (i.w_out, 768)):
-        pack[:, c0 : c0 + 256] = ref[...]
-    pack[:, 1024:] = i.columns[...]
     g_small.start()
     g_small.start_far()
+    g_out.start()
+    g_out.start_far()
     g_gate.start()
     g_up.start()
     g_down.start()
@@ -912,12 +944,14 @@
     g_gate.start_far()
     g_small.finish()
 
-    o.gains[...] = small[:, 1024:].astype(F32).T[:8, :]
+    o.gains[...] = small[:, 768:896].astype(F32).T[:8, :]
     for f in range(4):
-        head_cols[64 * f : 64 * f + 64, :] = small[288 * f : 288 * f + 64, 1024:].astype(F32)
+        head_cols[64 * f : 64 * f + 64, :] = small[288 * f : 288 * f + 64, 768:896].astype(F32)
     o.heads[...] = head_cols[...].T[:8, :]
-
-    @pl.loop(0, 16)
+    leave.gains.start()
+    leave.heads.start()
+
+    @pl.loop(0, 16, unroll=4)
     def _(b):
         at = pl.ds(pl.multiple_of(b * 16, 16), 16)
         normed[at, :] = normalize(i.tokens[at, :].astype(F32), o.gains[0:1, :]).astype(BF)
@@ -953,6 +987,7 @@
         n = normalize(o.q_proj[at, :], o.heads[4:5, :])
         o.queries[at, :] = turn(n, i.cosine[at, :], i.sine[at, :]).astype(BF)
 
+    g_out.forward()
     g_gate.across()
     g_up.start_far()
     for copy in sent:
@@ -967,6 +1002,8 @@
             for e in (2, 1, 3)
         ]
     transpose_into(o.normed_t, normed)
+    for copy in (leave.normed_t, leave.queries, leave.q_proj, leave.k_proj):
+        copy.start()
     for copy in sent_k:
         copy.wait_recv()
     g_gate.forward()
@@ -976,7 +1013,7 @@
     def _(b):
         at = pl.ds(pl.multiple_of(b * 64, 64), 64)
         query = o.queries[at, :]
-        seen = [i.key_pos[kb] <= i.query_pos[at, :] for kb in range(8)]
+        seen = [i.key_pos[kb] <= own_pos[at, :] for kb in range(8)]
         scores = [against(query, kv[kb, :, :HD]) * scale for kb in range(8)]
         top = jnp.max(jnp.where(seen[0], scores[0], -1e30), axis=-1, keepdims=True)
         for kb in range(1, 8):
@@ -993,6 +1030,8 @@
             probs[kb, at, :] = (scores[kb] * share).astype(BF)
 
     g_up.across()
+    g_out.finish()
+    leave.small.start()
     for copy in sent_z:
         copy.wait_recv()
     attn = plain(probs[0], kv[0, :, HD:])
@@ -1001,8 +1040,10 @@
     o.attn[...] = attn
     attn_low = attn.astype(BF)
     o.attn_low[...] = attn_low
+    for copy in (leave.kv, leave.lse, leave.attn, leave.attn_low):
+        copy.start()
     for h, rows in halves:
-        part[rows, :] = against(attn_low[rows], small[:, 768:1024]).astype(BF)
+        part[rows, :] = against(attn_low[rows], small[:, 896:]).astype(BF)
         firsts[h].start()
     g_up.forward()
     g_down.across()
@@ -1022,8 +1063,10 @@
 
     for h, rows in halves:
         firsts[h].finish()
-        pl.loop(8 * h, 8 * h + 8)(middle_rows)
+        pl.loop(8 * h, 8 * h + 8, unroll=4)(middle_rows)
     g_up.finish()
+    leave.branch.start()
+    leave.middle.start()
     for c0, c1 in TILES:
         gate = plain(normed[...], w_gate[:, c0:c1])
         up = plain(normed[...], w_up[:, c0:c1])
@@ -1033,6 +1076,7 @@
         act[:, c0:c1] = gelu
         rise = 0.7978845608028654 * (1.0 + 0.134145 * gate * gate)
         slope[:, c0:c1] = up * (0.5 * (1.0 + bend) + 0.5 * gate * (1.0 - bend * bend) * rise)
+    leave.hidden.start()
     g_down.forward()
     g_down.finish()
     for h, rows in halves:
@@ -1042,6 +1086,7 @@
             ).astype(BF)
         seconds[h].start()
     transpose_into(o.normed2_t, normed)
+    leave.normed2_t.start()
     for half in seconds:
         half.middle()
 
@@ -1055,43 +1100,30 @@
 
     for h, rows in halves:
         seconds[h].finish()
-        pl.loop(8 * h, 8 * h + 8)(last_rows)
+        pl.loop(8 * h, 8 * h + 8, unroll=4)(last_rows)
     o.dg3[...] = jnp.sum(accg[...], axis=0, keepdims=True)
     transpose_into(o.d_ffn_t, d_ffn)
+    for copy in (leave.out, leave.dg3, leave.d_ffn_t):
+        copy.start()
     for c0, c1 in TILES:
         d_hidden = plain(d_ffn[...], w_down[:, c0:c1])
         o.d_up[:, c0:c1] = (d_hidden * act[:, c0:c1]).astype(BF)
         o.d_gate[:, c0:c1] = (d_hidden * slope[:, c0:c1]).astype(BF)
+    leave.d_up.start()
+    leave.d_gate.start()
     for c0 in range(0, 1152, 384):
         o.x[:, c0 : c0 + 384] = (
             against(o.d_gate[...], w_gate[c0 : c0 + 384, :])
             + against(o.d_up[...], w_up[c0 : c0 + 384, :])
         ).astype(BF)
+    leave.x.start()
+    for copy in leave:
+        copy.wait()
     for copy in sent + sent_k + sent_z:
         copy.wait_send()
 
 
 def fore_call(ins, cid):
-    scratch = (
-        [pltpu.VMEM((1152, 1728), BF)] * 3
-        + [
-            pltpu.VMEM((256, 1728), F32),
-            pltpu.VMEM((256, 1728), F32),
-            pltpu.VMEM((256, 1152), BF),
-            pltpu.VMEM((256, 1152), BF),
-            pltpu.VMEM((8, 256, 256), BF),
-            pltpu.VMEM((256, 128), F32),
-            pltpu.VMEM((16, 1152), F32),
-            pltpu.SemaphoreType.DMA((4,)),
-        ]
-        + sems(24)
-        + sems(7)
-        + sems(7)
-        + sems(24)
-        + [pltpu.VMEM((256, 1152), BF)] * 2
-        + zsum_buffers(32) * 4
-        + [pltpu.VMEM((256, 1152), BF), pltpu.VMEM((288, 1152), BF)]
-    )
     shapes = ForeOut(
         out=((256, 1152), BF),
         small=((1152, 1152), BF),
@@ -1115,11 +1147,34 @@
         q_proj=((256, 256), F32),
         k_proj=((256, 256), F32),
     )
+    scratch = (
+        [pltpu.VMEM(*shape) for shape in shapes]
+        + [pltpu.SemaphoreType.DMA((len(shapes),))]
+        + [pltpu.VMEM((1152, 1728), BF)] * 3
+        + [
+            pltpu.VMEM((256, 1728), F32),
+            pltpu.VMEM((256, 1728), F32),
+            pltpu.VMEM((256, 1152), BF),
+            pltpu.VMEM((256, 1152), BF),
+            pltpu.VMEM((8, 256, 256), BF),
+            pltpu.VMEM((256, 128), F32),
+            pltpu.VMEM((16, 1152), F32),
+            pltpu.SemaphoreType.DMA((5,)),
+        ]
+        + sems(30)
+        + sems(7)
+        + sems(7)
+        + sems(24)
+        + [pltpu.VMEM((256, 1152), BF)] * 2
+        + zsum_buffers(32) * 4
+        + [pltpu.VMEM((256, 1152), BF), pltpu.VMEM((288, 1152), BF)]
+        + [pltpu.VMEM((128, 384), F32), pltpu.VMEM((256, 1), F32)]
+    )
     done = pl.pallas_call(
         fore_kernel,
         out_shape=[jax.ShapeDtypeStruct(*shape) for shape in shapes],
-        in_specs=[VM] * len(ins),
-        out_specs=[VM] * len(shapes),
+        in_specs=[HB if a.shape == (288, 1728) else VM for a in ins],
+        out_specs=[HB] * len(shapes),
         scratch_shapes=scratch,
         compiler_params=params(cid, 62),
         name="forward",
@@ -1196,10 +1251,6 @@
     span = rows // 2
     seq_len = rows * 8
 
-    columns = jnp.pad(
-        jnp.concatenate([gains.T, jnp.pad(head_gains.T, ((0, 288 - 64), (0, 0)))], axis=1),
-        ((0, 0), (0, 122)),
-    )
     offsets = jnp.arange(seq_len, dtype=jnp.int32)
     key_pos = (jnp.repeat(block_order, span, axis=1) * span + (offsets % span)[None, :])[0]
     query_pos = lax.dynamic_slice_in_dim(key_pos, cycle_index * rows, rows, 0)
@@ -1211,14 +1262,14 @@
         w_key=w_key,
         w_value=w_value,
         w_out=w_out.T,
-        columns=columns,
+        scales=gains,
+        head_scales=head_gains,
         w_gate=w_gate,
         w_up=w_up,
         w_down=w_down.T,
         cosine=cosine,
         sine=sine,
-        key_pos=key_pos.reshape(8, 1, rows),
-        query_pos=query_pos[:, None],
+        key_pos=key_pos.astype(F32).reshape(8, 1, rows),
     )
     held = fore_call(ins, 1)
     grad_tokens, sum_down, sum_gate, sum_up, sum_q, sum_o, sum_k, sum_v, last = back_call(
@@ -1241,7 +1292,6 @@
             queries=held.queries,
             kv=held.kv,
             key_pos=ins.key_pos,
-            query_pos=ins.query_pos,
             small=held.small,
             normed_t=held.normed_t,
             q_proj=held.q_proj,

time: 240 us -> 227 us (0.946)
  Pallas kernels: 234 us -> 223 us
    pallas_call x1, Pallas kernels: 129 us -> 124 us  [back_call(): pl.pallas_call(back_kernel, out_shape=[jax.ShapeDtypeStruct(*shape) for s...]
    pallas_call x1, Pallas kernels: 99.3 us -> 94.5 us  [fore_call(): pl.pallas_call(fore_kernel, out_shape=[jax.ShapeDtypeStruct(*shape) for s...]
where the time goes in v3:
time: 227 us
  Pallas kernels  223 us (98%)
  other arithmetic  2.55 us (1%)
    pallas_call x1, Pallas kernels, back_call(): pl.pallas_call(back_kernel, out_shape=[jax.ShapeDtypeStruct(*shape) for s...  124 us
    pallas_call x1, Pallas kernels, fore_call(): pl.pallas_call(fore_kernel, out_shape=[jax.ShapeDtypeStruct(*shape) for s...  94.5 us
    pallas_call x1, Pallas kernels, final_call(): pl.pallas_call(final_kernel, out_shape=[jax.ShapeDtypeStruct(shape, BF if...  5.05 us

profile of v3, /device:TPU:0, one launch (start us, length us, event | category | flops | bytes accessed | tf_op | source)
XLA Modules:
  0.0 226.9 jit_solution(11606079080994767764)
XLA Ops:
  0.7 0.7 multiply_reduce_fusion
  1.3 0.1 mul.79
  1.4 0.1 broadcast_in_dim.15
  1.5 0.6 fusion.2.refs_13_.refs_17_
  2.1 0.1 broadcast_in_dim.14
  2.2 1.2 multiply_sine_fusion
  3.4 94.5 %forward.1 = (bf16[256,1152]{1,0:T(8,128)(2,1)}, bf16[1152,1152]{1,0:T(8,128)(2,1)}, f32[8,1152]{1,0:T(8,128)}, f32[8,256]{1,0:T(8,128)}, bf16[256,1152]{1,0:T(8...) custom-call(bf16[256,1152]{1,0:T(8,128)(2,1)} %bitcast.13, ...), custom_call_target="tpu_custom_call" | custom-call | tf_op jit(solution)/shard_map/forward/pallas_call | solution.py:1173
  97.9 123.8 %backward.1 = (f32[256,1152]{1,0:T(8,128)}, bf16[288,1728]{1,0:T(8,128)(2,1)}, bf16[288,1728]{1,0:T(8,128)(2,1)}, bf16[288,1728]{1,0:T(8,128)(2,1)}, bf16[288,25...) custom-call(bf16[256,1152]{1,0:T(8,128)(2,1)} %get-tuple-element.53., ...), custom_call_target="tpu_custom_call" | custom-call | tf_op jit(solution)/shard_map/backward/pallas_call | solution.py:820
  221.7 5.0 %final.1 = (bf16[256,1152]{1,0:T(8,128)(2,1)}, f32[256,1152]{1,0:T(8,128)}, f32[288,1728]{1,0:T(8,128)}, f32[288,1728]{1,0:T(8,128)}, f32[288,1728]{1,0:T(8,128)...) custom-call(bf16[256,1152]{1,0:T(8,128)(2,1)} %get-tuple-element.52., ...), custom_call_target="tpu_custom_call" | custom-call | tf_op jit(solution)/shard_map/final/pallas_call | solution.py:1215
  (2 shorter events, 0.0 us)

commit v4 on v3

--- a/solution.py
+++ b/solution.py
@@ -199,7 +199,7 @@
             copy.wait_recv()
         own = self.rows(p.z)
 
-        @pl.loop(0, self.share // 16)
+        @pl.loop(0, self.share // 16, unroll=2)
         def _(i):
             at = pl.ds(pl.multiple_of(self.base + p.z * self.share + i * 16, 16), 16)
             to = pl.ds(pl.multiple_of(i * 16, 16), 16)
@@ -279,7 +279,7 @@
 
         else:
 
-            @pl.loop(0, 18)
+            @pl.loop(0, 18, unroll=3)
             def _(i):
                 at = pl.ds(pl.multiple_of(i * 16, 16), 16)
                 for j in (0, 1):
@@ -299,7 +299,7 @@
             copy.wait_recv()
         rest = self.n - cut
 
-        @pl.loop(0, 9)
+        @pl.loop(0, 9, unroll=3)
         def _(i):
             for h in (0, 1):
                 at = pl.ds(pl.multiple_of(h * 144 + i * 16, 16), 16)
@@ -326,7 +326,7 @@
                 )
 
     def sum_rows(self, dst, first, *more):
-        @pl.loop(0, 9)
+        @pl.loop(0, 9, unroll=3)
         def _(i):
             at = pl.ds(pl.multiple_of(i * 16, 16), 16)
             total = first[at, :].astype(F32)
@@ -396,7 +396,7 @@
         for copy in self.c5b + (self.c5 if self.direct else self.c5[1::2]):
             copy.wait_recv()
 
-        @pl.loop(0, 9)
+        @pl.loop(0, 9, unroll=3)
         def _(i):
             at = pl.ds(pl.multiple_of(i * 16, 16), 16)
             for h in (0, 1):

time: 227 us -> 227 us (level)
  no operation moved by 1% of the time
where the time goes in v4:
time: 227 us
  Pallas kernels  223 us (98%)
  other arithmetic  2.55 us (1%)
    pallas_call x1, Pallas kernels, back_call(): pl.pallas_call(back_kernel, out_shape=[jax.ShapeDtypeStruct(*shape) for s...  124 us
    pallas_call x1, Pallas kernels, fore_call(): pl.pallas_call(fore_kernel, out_shape=[jax.ShapeDtypeStruct(*shape) for s...  94.6 us
    pallas_call x1, Pallas kernels, final_call(): pl.pallas_call(final_kernel, out_shape=[jax.ShapeDtypeStruct(shape, BF if...  5.05 us

profile of v4, /device:TPU:0, one launch (start us, length us, event | category | flops | bytes accessed | tf_op | source)
XLA Modules:
  0.0 227.0 jit_solution(15144712452565528776)
XLA Ops:
  0.7 0.7 multiply_reduce_fusion
  1.3 0.1 mul.79
  1.4 0.1 broadcast_in_dim.15
  1.5 0.6 fusion.2.refs_13_.refs_17_
  2.1 0.1 broadcast_in_dim.14
  2.2 1.2 multiply_sine_fusion
  3.4 94.6 %forward.1 = (bf16[256,1152]{1,0:T(8,128)(2,1)}, bf16[1152,1152]{1,0:T(8,128)(2,1)}, f32[8,1152]{1,0:T(8,128)}, f32[8,256]{1,0:T(8,128)}, bf16[256,1152]{1,0:T(8...) custom-call(bf16[256,1152]{1,0:T(8,128)(2,1)} %bitcast.13, ...), custom_call_target="tpu_custom_call" | custom-call | tf_op jit(solution)/shard_map/forward/pallas_call | solution.py:1173
  98.1 123.7 %backward.1 = (f32[256,1152]{1,0:T(8,128)}, bf16[288,1728]{1,0:T(8,128)(2,1)}, bf16[288,1728]{1,0:T(8,128)(2,1)}, bf16[288,1728]{1,0:T(8,128)(2,1)}, bf16[288,25...) custom-call(bf16[256,1152]{1,0:T(8,128)(2,1)} %get-tuple-element.53., ...), custom_call_target="tpu_custom_call" | custom-call | tf_op jit(solution)/shard_map/backward/pallas_call | solution.py:820
  221.8 5.0 %final.1 = (bf16[256,1152]{1,0:T(8,128)(2,1)}, f32[256,1152]{1,0:T(8,128)}, f32[288,1728]{1,0:T(8,128)}, f32[288,1728]{1,0:T(8,128)}, f32[288,1728]{1,0:T(8,128)...) custom-call(bf16[256,1152]{1,0:T(8,128)(2,1)} %get-tuple-element.52., ...), custom_call_target="tpu_custom_call" | custom-call | tf_op jit(solution)/shard_map/final/pallas_call | solution.py:1215
  (2 shorter events, 0.0 us)
